TPU v7x, 32 devices: a whole 2x2x4 slice. The times are simulated.
32 devices in a mesh: tmpl: 8 (over z, x), sta: 4 (over y, core).
Axes of the slice: x: 2, y: 2, z: 4, core: 2. Of those that a mesh axis runs over, the one named last changes fastest.
Arguments:
- waveforms: bfloat16 [2048, 3, 1664], P(('tmpl', 'sta')), may hold values from -70 to 70, as said below
- templates: bfloat16 [256, 20, 3, 1024], P(('tmpl', 'sta')), may hold values from -0.5 to 1.5
- stations: int32 [256, 20], P(('tmpl', 'sta')), may hold values from 0 to 2047, as said below
- moveouts: int32 [256, 20], P(('tmpl', 'sta')), may hold values from 0 to 384
Outputs:
- stacks: float32 [256, 256], P(('tmpl', 'sta'))
- strongest: float32 [256], replicated
Inputs may be any that keep to these rules, and one draw needn't show every extreme that they name: Station s lies on device s // 64 in the order of tmpl+sta. Of the 160 entries of the templates on one device, at most 10 name stations of one device. `waveforms`: recorded traces of order one to tens.
All inputs are finite; a program needn't handle non-finite values.
Results may differ from a plain program's by a relative error of at most 0.0029.
Values may be sent and summed in bfloat16 or wider, within the bound.
No kernel may reach another device: no remote copies, remote signals or barrier semaphores. Data moves between devices by JAX's collectives and lax.ppermute only.
A program may use at most 64 MiB of HBM per device.

v0:
```python
import functools
import math

import jax
import jax.numpy as jnp
import ml_dtypes
import numpy as np
from jax import lax
from jax.experimental import pallas as pl
from jax.experimental.pallas import tpu as pltpu
from jax.sharding import PartitionSpec as P

LAGS = 256
HALF = "half"
GROUP = ("tmpl", "sta")
AXES = (HALF,) + GROUP
SOURCES = 8
LANES = 128
MIB = 1024 * 1024


def bits_of(limit):
    return max(1, (limit - 1).bit_length())


def split_table(table):
    high = table.astype(ml_dtypes.bfloat16)
    return high, (table - high.astype(np.float64)).astype(ml_dtypes.bfloat16)


def transform_table(piece):
    size = 2 * piece
    angle = 2.0 * np.pi * (np.arange(piece) + 0.5) / size
    phase = np.arange(piece)[:, None] * angle[None, :]
    forward = np.concatenate([np.cos(phase), -np.sin(phase)], axis=1)
    inverse = np.concatenate([np.cos(phase.T), -np.sin(phase.T)], axis=0) * (2.0 / size)
    return np.concatenate([*split_table(forward), np.concatenate(split_table(inverse), axis=1)], axis=0)


def edge_table(lag_count):
    sample = np.arange(lag_count)[:, None]
    lag = np.arange(lag_count)[None, :]
    return np.concatenate([sample >= lag, sample < lag], axis=0).astype(ml_dtypes.bfloat16)


def iota(shape, axis):
    return lax.broadcasted_iota(jnp.int32, shape, axis)


def dot(a, b):
    return jnp.dot(a, b, preferred_element_type=jnp.float32)


def exact_dot(a, b):
    return jnp.dot(a, b, precision=lax.Precision.HIGHEST, preferred_element_type=jnp.float32)


def entry_lanes(tpl_count, slot_count):
    pairs = tpl_count * slot_count
    first = iota((slot_count, pairs), 0) * tpl_count
    entry = iota((slot_count, pairs), 1)
    spread = jnp.where((entry >= first) & (entry < first + tpl_count), 1.0, 0.0)
    start = jnp.sum(spread * first.astype(jnp.float32), axis=0, keepdims=True)
    return spread, iota((1, pairs), 1).astype(jnp.float32) - start


def as_lanes(values, spread, place, tpl_count):
    owners = values.shape[0] // tpl_count
    pairs = spread.shape[1]
    wide = exact_dot(values.astype(jnp.float32), spread).reshape(owners, tpl_count, pairs)
    own = iota((1, tpl_count, pairs), 1).astype(jnp.float32) == place.reshape(1, 1, pairs)
    return jnp.sum(jnp.where(own, wide, 0.0), axis=1)


def count_before(hits):
    pairs = hits.shape[1]
    earlier = jnp.where(iota((pairs, pairs), 0) < iota((pairs, pairs), 1), 1.0, 0.0)
    return dot(hits.astype(jnp.bfloat16), earlier.astype(jnp.bfloat16))


def list_kernel(cfg, half_ref, stations_ref, moveouts_ref, codes_ref, goal_ref):
    tpl_count, slot_count = stations_ref.shape
    pairs = tpl_count * slot_count
    devices, group, halves = cfg["devices"], cfg["group"], cfg["halves"]
    station_dev, rows, capacity = cfg["station_dev"], cfg["rows"], cfg["capacity"]
    spread, place = entry_lanes(tpl_count, slot_count)
    station = as_lanes(stations_ref[...], spread, place, tpl_count)
    shift = as_lanes(moveouts_ref[...], spread, place, tpl_count)
    device = jnp.floor((station + 0.5) * (1.0 / station_dev))
    onehot = jnp.where(iota((devices, pairs), 0).astype(jnp.float32) == device, 1.0, 0.0)
    rank = jnp.sum(onehot * count_before(onehot), axis=0, keepdims=True)
    half = jnp.floor((device + 0.5) * (1.0 / group))
    away = jnp.where(half == half_ref[0].astype(jnp.float32), 0.0, 1.0)
    place_of = (device - half * group) * halves + away
    goal_ref[...] = jnp.where(rank < float(capacity), place_of * rows + rank, -float(group * halves * rows))

    row = station - device * station_dev
    code = ((place + 1.0) * (1 << cfg["row_bits"]) + row) * (1 << cfg["shift_bits"]) + shift
    marked = jnp.where(iota((group * halves, pairs), 0).astype(jnp.float32) == place_of, code, 0.0)
    at_rank = jnp.where(iota((LANES, pairs), 0).astype(jnp.float32) == rank, 1.0, 0.0)
    codes = lax.dot_general(
        marked,
        at_rank,
        (((1,), (1,)), ((), ())),
        precision=lax.Precision.HIGHEST,
        preferred_element_type=jnp.float32,
    )
    codes_ref[...] = codes.astype(jnp.int32)


def pack_kernel(cfg, goal_ref, templates_hbm, packed_hbm, raw_ref, shapes_ref, packed_ref, in_sem, out_sems):
    load = pltpu.make_async_copy(templates_hbm, raw_ref, in_sem)
    load.start()
    goal = goal_ref[...]
    pairs = goal.shape[1]
    comps, length = raw_ref.shape[1], raw_ref.shape[3]
    load.wait()
    for c in range(comps):
        values = raw_ref[:, c].astype(jnp.float32).reshape(pairs, length)
        centred = values - jnp.mean(values, axis=-1, keepdims=True)
        spread_c = jnp.sqrt(jnp.mean(centred * centred, axis=-1, keepdims=True) + 1e-05)
        shapes_ref[c] = (centred * (1.0 / spread_c)).astype(jnp.bfloat16)

    tiles = out_sems.shape[0]
    tile = packed_ref.shape[0] // tiles
    copies = []
    for step in range(tiles):
        line = iota((tile, pairs), 0).astype(jnp.float32) + float(step * tile)
        total = jnp.zeros((tile, length), jnp.float32)
        for c in range(comps):
            pick = jnp.where(line == goal + float(c * cfg["capacity"]), 1.0, 0.0).astype(jnp.bfloat16)
            total = total + dot(pick, shapes_ref[c])
        part = pl.ds(step * tile, tile)
        packed_ref[part, :] = total.astype(jnp.bfloat16)
        copies.append(pltpu.make_async_copy(packed_ref.at[part], packed_hbm.at[part], out_sems.at[step]))
        copies[-1].start()
    for copy in copies:
        copy.wait()


def tile_lines(cfg, codes):
    capacity, rows, comps, halves = cfg["capacity"], cfg["rows"], cfg["comps"], cfg["halves"]
    blocks = SOURCES * halves
    tile = blocks * rows
    line = iota((blocks, rows, 1), 1).reshape(tile, 1)
    block = iota((blocks, rows, 1), 0).reshape(tile, 1)
    comp = jnp.zeros((tile, 1), jnp.int32)
    for c in range(1, comps + 1):
        comp = comp + jnp.where(line >= c * capacity, 1, 0)
    slot = line - comp * capacity
    owner = jnp.zeros((tile, 1), jnp.int32)
    for k in range(1, SOURCES):
        owner = owner + jnp.where(block >= k * halves, 1, 0)
    repeated = codes.astype(jnp.float32).reshape(blocks, 1, LANES)
    repeated = jnp.broadcast_to(repeated, (blocks, rows, LANES)).reshape(tile, LANES)
    chosen = (iota((tile, LANES), 1) == slot) & (comp < comps)
    code = jnp.sum(jnp.where(chosen, repeated, 0.0), axis=1, keepdims=True).astype(jnp.int32)
    shift_bits, row_bits = cfg["shift_bits"], cfg["row_bits"]
    shift = code & ((1 << shift_bits) - 1)
    row = lax.shift_right_logical(code, shift_bits) & ((1 << row_bits) - 1)
    tpl = lax.shift_right_logical(code, shift_bits + row_bits) - 1
    goal = ((block - owner * halves) * comps + comp) * cfg["station_dev"] + row
    return shift, jnp.where(tpl >= 0, goal, -1), jnp.where(tpl >= 0, owner * cfg["tpl_count"] + tpl, -1)


def cut_traces(cfg, shift, goal, waves):
    tile, seg_len, shift_bits = shift.shape[0], cfg["seg_len"], cfg["shift_bits"]
    pick = jnp.where(iota((tile, waves.shape[0]), 1) == goal, 1.0, 0.0).astype(jnp.bfloat16)
    x = dot(pick, waves).astype(jnp.bfloat16)

    def choose(step, moved, still):
        flag = jnp.where((shift & step) != 0, 1.0, 0.0)
        return moved * flag.astype(jnp.bfloat16) + still * (1.0 - flag).astype(jnp.bfloat16)

    for bit in range(shift_bits - 1, 6, -1):
        step = 1 << bit
        width = seg_len + step
        if x.shape[1] < width + step:
            x = jnp.concatenate([x, jnp.zeros((tile, width + step - x.shape[1]), jnp.bfloat16)], axis=1)
        x = choose(step, x[:, step : step + width], x[:, :width])
    for bit in range(min(shift_bits, 7) - 1, -1, -1):
        step = 1 << bit
        x = choose(step, pltpu.roll(x, x.shape[1] - step, 1), x)
    return x[:, :seg_len]


def line_sums(cfg, column):
    groups = SOURCES * cfg["tpl_count"]
    return jnp.where(iota((column.shape[0], groups), 1) == column, 1.0, 0.0).T.astype(jnp.bfloat16)


def levels_scale(cfg, narrow, edges):
    length = cfg["length"]
    ends = jnp.concatenate([narrow[:, :LAGS], narrow[:, length:]], axis=1).astype(jnp.float32)
    ends = ends * ends
    high = ends.astype(jnp.bfloat16)
    low = (ends - high.astype(jnp.float32)).astype(jnp.bfloat16)
    middle = narrow[:, LAGS:length].astype(jnp.float32)
    energy = dot(high, edges) + dot(low, edges) + jnp.sum(middle * middle, axis=1, keepdims=True)
    return 1.0 / (length * jnp.sqrt(energy * (1.0 / length) + 1e-05))


def shape_spectra(shapes, forward):
    spectra = []
    for h in range(shapes.shape[1] // LAGS):
        part = shapes[:, h * LAGS : (h + 1) * LAGS]
        mine = dot(jnp.concatenate([part, part], axis=1), forward)
        spectra.append((mine[:, :LAGS], mine[:, LAGS:]))
    return spectra


def match_lines(mine, theirs, scale, inverse):
    real = imag = 0.0
    for (mine_r, mine_i), (theirs_r, theirs_i) in zip(mine, theirs):
        real = real + (theirs_r * mine_r + theirs_i * mine_i)
        imag = imag + (theirs_i * mine_r - theirs_r * mine_i)
    product = jnp.concatenate([real, imag], axis=1)
    high = product.astype(jnp.bfloat16)
    low = (product - high.astype(jnp.float32)).astype(jnp.bfloat16)
    return dot(jnp.concatenate([high, high, low], axis=1), inverse) * scale


def sum_lines(sums, left):
    total = 0.0
    for _ in range(3):
        part = left.astype(jnp.bfloat16)
        left = left - part.astype(jnp.float32)
        total = total + dot(sums, part)
    return total


def tables_of(table_ref):
    back = table_ref[2 * LAGS :, :]
    high, low = back[:, :LAGS], back[:, LAGS:]
    return table_ref[: 2 * LAGS, :], jnp.concatenate([high, low, high], axis=0)


def trace_kernel(cfg, codes_ref, *refs):
    waves_refs, (table_ref, edges_ref, kept_ref, sums_ref) = refs[:-4], refs[-4:]
    shift, goal, column = tile_lines(cfg, codes_ref[...])
    waves = [ref[...].reshape(-1, ref.shape[2]) for ref in waves_refs]
    narrow = cut_traces(cfg, shift, goal, jnp.concatenate(waves, axis=0))
    kept_ref[:, 2 * cfg["length"] :] = levels_scale(cfg, narrow, edges_ref[...])
    sums_ref[...] = line_sums(cfg, column)

    sign = (1 - 2 * (iota((1, LAGS), 1) & 1)).astype(jnp.float32)
    before = None
    for h in range(cfg["length"] // LAGS + 1):
        part = narrow[:, h * LAGS : (h + 1) * LAGS]
        here = dot(jnp.concatenate([part, part], axis=1), table_ref[...])
        here = here[:, :LAGS], here[:, LAGS:]
        if before is not None:
            kept_ref[:, (2 * h - 2) * LAGS : (2 * h - 1) * LAGS] = before[0] + sign * here[1]
            kept_ref[:, (2 * h - 1) * LAGS : 2 * h * LAGS] = before[1] - sign * here[0]
        before = here


def match_kernel(tiles, shapes_hbm, kept_hbm, sums_hbm, table_hbm, sent_ref, *scratch):
    shapes_ref, kept_ref, sums_ref, table_ref, sems = scratch
    tile = shapes_ref.shape[0] // tiles
    groups = sent_ref.shape[0] // tiles
    length = shapes_ref.shape[1]
    copies = []

    def fetch(source, buffer, part=None):
        if part is not None:
            source, buffer = source.at[part], buffer.at[part]
        copies.append(pltpu.make_async_copy(source, buffer, sems.at[len(copies)]))
        copies[-1].start()
        return copies[-1]

    lines = [pl.ds(t * tile, tile) for t in range(tiles)]
    halves = [pl.ds(q * 2 * LAGS, 2 * LAGS) for q in range(2)]
    forward = fetch(table_hbm, table_ref, halves[0])
    shapes, kept = [], []
    for t in range(tiles):
        shapes.append(fetch(shapes_hbm, shapes_ref, lines[t]))
        kept.append(fetch(kept_hbm, kept_ref, lines[t]))
        if t == 0:
            inverse = fetch(table_hbm, table_ref, halves[1])
            sums = fetch(sums_hbm, sums_ref)
    forward.wait()
    for t in range(tiles):
        shapes[t].wait()
        mine = shape_spectra(shapes_ref[lines[t], :], table_ref[: 2 * LAGS, :])
        kept[t].wait()
        theirs = kept_ref[lines[t], :]
        spectra = [
            (theirs[:, 2 * h * LAGS : (2 * h + 1) * LAGS], theirs[:, (2 * h + 1) * LAGS : (2 * h + 2) * LAGS])
            for h in range(length // LAGS)
        ]
        if t == 0:
            for copy in (inverse, sums):
                copy.wait()
        left = match_lines(mine, spectra, theirs[:, 2 * length :], tables_of(table_ref)[1])
        ends = pl.ds(t * groups, groups)
        sent_ref[ends, :] = sum_lines(sums_ref[ends, :], left)


def stack_kernel(factor, parts_ref, stacks_ref, top_ref):
    stacks = jnp.sum(parts_ref[...], axis=0) * factor
    stacks_ref[...] = stacks
    top_ref[...] = jnp.broadcast_to(jnp.max(stacks, axis=0, keepdims=True), top_ref.shape)


def body(waveforms, templates, stations, moveouts):
    devices, group, halves = lax.axis_size(AXES), lax.axis_size(GROUP), lax.axis_size(HALF)
    tpl_count, slot_count = stations.shape
    comps, length = templates.shape[2:]
    station_dev, _, samples = waveforms.shape
    seg_len = length + LAGS
    pairs = tpl_count * slot_count
    capacity = (2 * pairs + devices - 1) // devices
    rows = -(-comps * capacity // 16) * 16
    cfg = dict(
        devices=devices,
        group=group,
        halves=halves,
        station_dev=station_dev,
        tpl_count=tpl_count,
        comps=comps,
        capacity=capacity,
        rows=rows,
        length=length,
        seg_len=seg_len,
        shift_bits=bits_of(samples - seg_len + 1),
        row_bits=bits_of(station_dev),
    )
    table = jnp.asarray(transform_table(LAGS))
    edges = jnp.asarray(edge_table(LAGS))
    tiles = group // SOURCES
    tile = SOURCES * halves * rows
    lines = group * halves * rows
    sums_tile = SOURCES * tpl_count
    kept_len = 2 * length + LAGS
    whole = pl.BlockSpec(memory_space=pltpu.VMEM)
    anywhere = pl.BlockSpec(memory_space=pl.ANY)
    params = pltpu.CompilerParams(vmem_limit_bytes=60 * MIB)
    by_slot = templates.transpose(1, 2, 0, 3)
    waves = waveforms.transpose(1, 0, 2)
    half = lax.axis_index(HALF).reshape(1)

    def work(flops, size):
        return pl.CostEstimate(flops=flops, bytes_accessed=size, transcendentals=0)

    def exchange(x, axes):
        return lax.all_to_all(x, axes, split_axis=0, concat_axis=0, tiled=True)

    def same(shape):
        return pl.BlockSpec(shape, lambda i: (0,) * len(shape))

    def tiled(*shape):
        return pl.BlockSpec(shape, lambda i: (i, 0))

    traces = [waves] + [lax.ppermute(waves, HALF, [(0, 1), (1, 0)])] * (halves - 1)
    codes, goal = pl.pallas_call(
        functools.partial(list_kernel, cfg),
        out_shape=[
            jax.ShapeDtypeStruct((group * halves, LANES), jnp.int32),
            jax.ShapeDtypeStruct((1, pairs), jnp.float32),
        ],
        in_specs=[pl.BlockSpec(memory_space=pltpu.SMEM), whole, whole],
        out_specs=[whole, whole],
        compiler_params=params,
        cost_estimate=work(1, 1),
        name="lists",
    )(half, stations, moveouts)
    codes = exchange(codes.reshape(group, halves, LANES), GROUP).reshape(group * halves, LANES)

    pack_tiles = 4
    packed = pl.pallas_call(
        functools.partial(pack_kernel, cfg),
        out_shape=jax.ShapeDtypeStruct((lines, length), jnp.bfloat16),
        in_specs=[whole, anywhere],
        out_specs=anywhere,
        scratch_shapes=[
            pltpu.VMEM(by_slot.shape, jnp.bfloat16),
            pltpu.VMEM((comps, pairs, length), jnp.bfloat16),
            pltpu.VMEM((lines, length), jnp.bfloat16),
            pltpu.SemaphoreType.DMA,
            pltpu.SemaphoreType.DMA((pack_tiles,)),
        ],
        compiler_params=params,
        cost_estimate=work(5 * 10**9, 1),
        name="pack",
    )(goal, by_slot)
    codes, packed = lax.optimization_barrier((codes, packed))
    arrived = exchange(packed.reshape(group, halves * rows, length), GROUP).reshape(lines, length)

    kept, sums = pl.pallas_call(
        functools.partial(trace_kernel, cfg),
        grid=(tiles,),
        out_shape=[
            jax.ShapeDtypeStruct((lines, kept_len), jnp.float32),
            jax.ShapeDtypeStruct((group * tpl_count, tile), jnp.bfloat16),
        ],
        in_specs=[tiled(SOURCES * halves, LANES)]
        + [same(waves.shape)] * halves
        + [same((2 * LAGS, 2 * LAGS)), same(edges.shape)],
        out_specs=[tiled(tile, kept_len), tiled(sums_tile, tile)],
        compiler_params=params,
        cost_estimate=work(10**12, 1),
        name="traces",
    )(codes, *traces, table, edges)
    operands = (arrived, kept, sums, table)
    sent = pl.pallas_call(
        functools.partial(match_kernel, tiles),
        out_shape=jax.ShapeDtypeStruct((group * tpl_count, LAGS), jnp.float32),
        in_specs=[anywhere] * len(operands),
        out_specs=whole,
        scratch_shapes=[pltpu.VMEM(x.shape, x.dtype) for x in operands]
        + [pltpu.SemaphoreType.DMA((3 + 2 * tiles,))],
        compiler_params=pltpu.CompilerParams(vmem_limit_bytes=57 * MIB),
        name="match",
    )(*operands)

    parts = exchange(sent.reshape(group, tpl_count, LAGS), GROUP)
    stacks, top = pl.pallas_call(
        functools.partial(stack_kernel, math.sqrt(length / (comps * slot_count))),
        out_shape=[
            jax.ShapeDtypeStruct((tpl_count, LAGS), jnp.float32),
            jax.ShapeDtypeStruct((devices, 1, LAGS), jnp.float32),
        ],
        in_specs=[whole],
        out_specs=[whole, whole],
        compiler_params=pltpu.CompilerParams(vmem_limit_bytes=16 * MIB),
        name="stack",
    )(parts)
    return stacks, jnp.max(exchange(top, AXES), axis=(0, 1))


def solution(mesh):
    slow, fast = (mesh.shape[name] for name in GROUP)
    halves = 2 if slow % 2 == 0 else 1
    split = jax.sharding.Mesh(mesh.devices.reshape(halves, slow // halves, fast), AXES)
    placed = (
        P(AXES, None, None),
        P(AXES, None, None, None),
        P(AXES, None),
        P(AXES, None),
    )
    return jax.shard_map(body, mesh=split, in_specs=placed, out_specs=(P(AXES, None), P()), check_vma=False)
```

profile of v0, /device:TPU:0, one launch (start us, length us, event | category | flops | bytes accessed | tf_op | source)
XLA Modules:
  0.0 90.9 jit_solution(9412465723059770681)
XLA Ops:
  0.6 4.1 %collective-permute-start = (bf16[3,64,1664]{2,1,0:T(8,128)(2,1)}, bf16[3,64,1664]{2,1,0:T(8,128)(2,1)S(1)}, u32[]{:S(2)}, u32[]{:S(2)}) collective-permute-start(bf16[3,64,1664]{2,1,0:T(8,128)(2,1)} %bitcast.13), channel_id=1, source_target_pairs={{0,16},{16,0},{1,17},{17,1},{2,18},{18,2},{3,19},{19,3},{4,20},{20... | collective-permute-start | bytes 1916936 | tf_op jit(solution)/shard_map/ppermute | solution.py:355
  4.7 1.8 %lists.1 = (s32[32,128]{1,0:T(8,128)}, f32[1,160]{1,0:T(1,128)}) custom-call(s32[1]{0:T(128)} %bitcast.half_ref, s32[8,20]{1,0:T(8,128)} %stations_ref.1, s32[8,20]{1,0:T(8,128)} %moveouts_ref.1), custom_call_target="tpu_custom_call" | custom-call | flops 1 | bytes 1 | tf_op jit(solution)/shard_map/lists/pallas_call | solution.py:356
  6.6 4.8 %all-to-all-start = ((s32[16,2,128]{2,1,0:T(2,128)}), s32[16,2,128]{2,1,0:T(2,128)S(1)}, u32[]{:S(2)}, u32[]{:S(2)}) async-start(s32[16,2,128]{2,1,0:T(2,128)} %bitcast.11), calls=%async_computation | async-start | bytes 32768 | tf_op jit(solution)/shard_map/all_to_all | solution.py:347
  11.4 4.9 %pack.1 = bf16[1024,1024]{1,0:T(8,128)(2,1)} custom-call(f32[1,160]{1,0:T(1,128)} %get-tuple-element.11.goal_ref, bf16[20,3,8,1024]{3,2,1,0:T(8,128)(2,1)} %bitcast.12), custom_call_target="tpu_custom_call" | custom-call | flops 5000000000 | bytes 1 | tf_op jit(solution)/shard_map/pack/pallas_call | solution.py:371
  16.3 2.5 %all-to-all-done = s32[16,2,128]{2,1,0:T(2,128)S(1)} async-done(((s32[16,2,128]{2,1,0:T(2,128)}), s32[16,2,128]{2,1,0:T(2,128)S(1)}, u32[]{:S(2)}, u32[]{:S(2)}) %all-to-all-start) | async-done | bytes 16416 | tf_op jit(solution)/shard_map/all_to_all | solution.py:347
  18.8 0.0 copy-start
  18.8 0.6 copy-done
  19.4 5.8 %all-to-all-start.1 = ((bf16[16,64,1024]{2,1,0:T(8,128)(2,1)}), bf16[16,64,1024]{2,1,0:T(8,128)(2,1)}, u32[]{:S(2)}, u32[]{:S(2)}) async-start(bf16[16,64,1024]{2,1,0:T(8,128)(2,1)} %bitcast.8), calls=%async_computation.1 | async-start | bytes 4194304 | tf_op jit(solution)/shard_map/all_to_all | solution.py:347
  25.2 7.9 %collective-permute-done.refs_1_ = bf16[3,64,1664]{2,1,0:T(8,128)(2,1)S(1)} collective-permute-done((bf16[3,64,1664]{2,1,0:T(8,128)(2,1)}, bf16[3,64,1664]{2,1,0:T(8,128)(2,1)S(1)}, u32[]{:S(2)}, u32[]{:S(2)}) %collective-permute-start) | collective-permute-done | bytes 639008 | tf_op jit(solution)/shard_map/ppermute | solution.py:355
  33.1 0.0 copy-start.1
  33.1 0.8 copy-done.1
  34.0 14.2 %traces.1 = (f32[1024,2304]{1,0:T(8,128)}, bf16[128,512]{1,0:T(8,128)(2,1)}) custom-call(s32[32,128]{1,0:T(8,128)} %bitcast.10, bf16[3,64,1664]{2,1,0:T(8,128)(2,1)} %bitcast.14, bf16[3,64,1664]{2,1,0:T(8,128)(2,1)} %copy-done.1, bf16[1024,512]{1,0:T(8,128)(2,1)} %constant.12.clone.refs_2_.table_hbm, bf16[512,256]{1,0:T(8,128)(2,1)} %constant.13.clone.refs_3_), custom_call_target="tpu_custom_call" | custom-call | flops 999999995904 | bytes 1 | tf_op jit(solution)/shard_map/traces/pallas_call | solution.py:390
  48.2 11.1 %all-to-all-done.1 = bf16[16,64,1024]{2,1,0:T(8,128)(2,1)} async-done(((bf16[16,64,1024]{2,1,0:T(8,128)(2,1)}), bf16[16,64,1024]{2,1,0:T(8,128)(2,1)}, u32[]{:S(2)}, u32[]{:S(2)}) %all-to-all-start.1) | async-done | bytes 2097184 | tf_op jit(solution)/shard_map/all_to_all | solution.py:347
  59.2 8.9 %match.1 = f32[128,256]{1,0:T(8,128)} custom-call(bf16[1024,1024]{1,0:T(8,128)(2,1)} %bitcast.5.shapes_hbm, f32[1024,2304]{1,0:T(8,128)} %get-tuple-element.14.kept_hbm, bf16[128,512]{1,0:T(8,128)(2,1)} %get-tuple-element.15.sums_hbm, bf16[1024,512]{1,0:T(8,128)(2,1)} %constant.12.clone.refs_2_.table_hbm), custom_call_target="tpu_custom_call" | custom-call | tf_op jit(solution)/shard_map/match/pallas_call | solution.py:406
  68.1 10.4 %all_to_all.20.parts_ref = f32[16,8,256]{2,1,0:T(8,128)S(1)} all-to-all(f32[16,8,256]{2,1,0:T(8,128)} %bitcast.9), channel_id=1, replica_groups=mesh['half'=2,'tmpl'=4,'sta'=4] {'tmpl','sta'}, dimensions={0} | all-to-all | bytes 262144 | tf_op jit(solution)/shard_map/all_to_all | solution.py:347
  78.5 0.6 stack.1
  79.1 11.2 %all_to_all.21 = f32[32,1,256]{2,1,0:T(1,128)S(1)} all-to-all(f32[32,1,256]{2,1,0:T(1,128)S(1)} %get-tuple-element.17), channel_id=1, replica_groups=mesh['half'=2,'tmpl'=4,'sta'=4] {'half','tmpl','sta'}, dimensions={0} | all-to-all | bytes 65536 | tf_op jit(solution)/shard_map/all_to_all | solution.py:347
  90.3 0.6 reduce_max.9
Async XLA Ops:
  0.6 32.5 %collective-permute-start = (bf16[3,64,1664]{2,1,0:T(8,128)(2,1)}, bf16[3,64,1664]{2,1,0:T(8,128)(2,1)S(1)}, u32[]{:S(2)}, u32[]{:S(2)}) collective-permute-start(bf16[3,64,1664]{2,1,0:T(8,128)(2,1)} %bitcast.13), channel_id=1, source_target_pairs={{0,16},{16,0},{1,17},{17,1},{2,18},{18,2},{3,19},{19,3},{4,20},{20... | collective-permute-start | bytes 1916936 | tf_op jit(solution)/shard_map/ppermute | solution.py:355
  6.6 12.3 %all-to-all-start = ((s32[16,2,128]{2,1,0:T(2,128)}), s32[16,2,128]{2,1,0:T(2,128)S(1)}, u32[]{:S(2)}, u32[]{:S(2)}) async-start(s32[16,2,128]{2,1,0:T(2,128)} %bitcast.11), calls=%async_computation | async-start | bytes 32768 | tf_op jit(solution)/shard_map/all_to_all | solution.py:347
  18.8 0.6 copy-start
  19.4 39.8 %all-to-all-start.1 = ((bf16[16,64,1024]{2,1,0:T(8,128)(2,1)}), bf16[16,64,1024]{2,1,0:T(8,128)(2,1)}, u32[]{:S(2)}, u32[]{:S(2)}) async-start(bf16[16,64,1024]{2,1,0:T(8,128)(2,1)} %bitcast.8), calls=%async_computation.1 | async-start | bytes 4194304 | tf_op jit(solution)/shard_map/all_to_all | solution.py:347
  33.1 0.8 copy-start.1
where the time goes:
time: 91.4 us; the launch traced here: 90.9 us
  Pallas kernels  30.4 us (33%)
  blocking collectives  21.6 us (24%)
  waiting for transfers between devices  21.4 us (23%)
  starting transfers between devices  14.7 us (16%)
  local copies, waits for them, and re-layouts  1.44 us (2%)
    all_to_all x2, blocking collectives, exchange(): return lax.all_to_all(x, axes, split_axis=0, concat_axis=0, tiled=True)  21.6 us
    pallas_call x1, Pallas kernels, body(): pl.pallas_call(functools.partial(trace_kernel, cfg), grid=(tiles,), out_s...  14.2 us
    all_to_all x2, waiting for transfers between devices, exchange(): return lax.all_to_all(x, axes, split_axis=0, concat_axis=0, tiled=True)  13.5 us
    all_to_all x2, starting transfers between devices, exchange(): return lax.all_to_all(x, axes, split_axis=0, concat_axis=0, tiled=True)  10.6 us
    pallas_call x1, Pallas kernels, body(): pl.pallas_call(functools.partial(match_kernel, tiles), out_shape=jax.Shap...  8.86 us
    ppermute x1, waiting for transfers between devices, body(): lax.ppermute(waves, HALF, [(0, 1), (1, 0)])  7.91 us
    pallas_call x1, Pallas kernels, body(): pl.pallas_call(functools.partial(pack_kernel, cfg), out_shape=jax.ShapeDt...  4.93 us
    ppermute x1, starting transfers between devices, body(): lax.ppermute(waves, HALF, [(0, 1), (1, 0)])  4.1 us
  transfers between devices with their start and end apart: 3, of which 3 were waited for; matrix products, arithmetic and copies ran while one was open for 0% of the time, Pallas kernels for 23%

commit v1 on v0

--- a/solution.py
+++ b/solution.py
@@ -15,7 +15,6 @@
 GROUP = ("tmpl", "sta")
 AXES = (HALF,) + GROUP
 SOURCES = 8
-LANES = 128
 MIB = 1024 * 1024
 
 
@@ -78,41 +77,31 @@
     return dot(hits.astype(jnp.bfloat16), earlier.astype(jnp.bfloat16))
 
 
-def list_kernel(cfg, half_ref, stations_ref, moveouts_ref, codes_ref, goal_ref):
+def list_kernel(cfg, stations_ref, moveouts_ref, lists_ref):
+    lists = stations_ref[...] * (1 << cfg["shift_bits"]) + moveouts_ref[...]
+    group, tpl_count, _ = lists_ref.shape
+    slot_count = lists.shape[1]
+    lists_ref[:, :, :slot_count] = jnp.broadcast_to(lists.reshape(1, tpl_count, slot_count), (group, tpl_count, slot_count))
+
+
+def pack_kernel(
+    cfg, half_ref, stations_ref, templates_hbm, packed_hbm, raw_ref, shapes_ref, packed_ref, in_sem, out_sems
+):
+    load = pltpu.make_async_copy(templates_hbm, raw_ref, in_sem)
+    load.start()
     tpl_count, slot_count = stations_ref.shape
     pairs = tpl_count * slot_count
-    devices, group, halves = cfg["devices"], cfg["group"], cfg["halves"]
-    station_dev, rows, capacity = cfg["station_dev"], cfg["rows"], cfg["capacity"]
+    devices, group, halves, rows = cfg["devices"], cfg["group"], cfg["halves"], cfg["rows"]
     spread, place = entry_lanes(tpl_count, slot_count)
     station = as_lanes(stations_ref[...], spread, place, tpl_count)
-    shift = as_lanes(moveouts_ref[...], spread, place, tpl_count)
-    device = jnp.floor((station + 0.5) * (1.0 / station_dev))
+    device = jnp.floor((station + 0.5) * (1.0 / cfg["station_dev"]))
     onehot = jnp.where(iota((devices, pairs), 0).astype(jnp.float32) == device, 1.0, 0.0)
     rank = jnp.sum(onehot * count_before(onehot), axis=0, keepdims=True)
     half = jnp.floor((device + 0.5) * (1.0 / group))
     away = jnp.where(half == half_ref[0].astype(jnp.float32), 0.0, 1.0)
-    place_of = (device - half * group) * halves + away
-    goal_ref[...] = jnp.where(rank < float(capacity), place_of * rows + rank, -float(group * halves * rows))
-
-    row = station - device * station_dev
-    code = ((place + 1.0) * (1 << cfg["row_bits"]) + row) * (1 << cfg["shift_bits"]) + shift
-    marked = jnp.where(iota((group * halves, pairs), 0).astype(jnp.float32) == place_of, code, 0.0)
-    at_rank = jnp.where(iota((LANES, pairs), 0).astype(jnp.float32) == rank, 1.0, 0.0)
-    codes = lax.dot_general(
-        marked,
-        at_rank,
-        (((1,), (1,)), ((), ())),
-        precision=lax.Precision.HIGHEST,
-        preferred_element_type=jnp.float32,
-    )
-    codes_ref[...] = codes.astype(jnp.int32)
-
-
-def pack_kernel(cfg, goal_ref, templates_hbm, packed_hbm, raw_ref, shapes_ref, packed_ref, in_sem, out_sems):
-    load = pltpu.make_async_copy(templates_hbm, raw_ref, in_sem)
-    load.start()
-    goal = goal_ref[...]
-    pairs = goal.shape[1]
+    goal = ((device - half * group) * halves + away) * rows + rank
+    goal = jnp.where(rank < float(cfg["capacity"]), goal, -float(group * halves * rows))
+
     comps, length = raw_ref.shape[1], raw_ref.shape[3]
     load.wait()
     for c in range(comps):
@@ -138,29 +127,48 @@
         copy.wait()
 
 
-def tile_lines(cfg, codes):
+def tile_lines(cfg, here, lists):
     capacity, rows, comps, halves = cfg["capacity"], cfg["rows"], cfg["comps"], cfg["halves"]
-    blocks = SOURCES * halves
-    tile = blocks * rows
-    line = iota((blocks, rows, 1), 1).reshape(tile, 1)
-    block = iota((blocks, rows, 1), 0).reshape(tile, 1)
+    station_dev, shift_bits, row_bits = cfg["station_dev"], cfg["shift_bits"], cfg["row_bits"]
+    tpl_count, slot_count = cfg["tpl_count"], cfg["slot_count"]
+    lists = lists[:, :slot_count]
+    pairs = tpl_count * slot_count
+    tile = SOURCES * halves * rows
+    spread, place = entry_lanes(tpl_count, slot_count)
+    station = as_lanes(lax.shift_right_logical(lists, shift_bits), spread, place, tpl_count)
+    shift = as_lanes(lists & ((1 << shift_bits) - 1), spread, place, tpl_count)
+
+    def per_line(parts):
+        wide = [jnp.broadcast_to(x.reshape(SOURCES, 1, pairs), (SOURCES, rows, pairs)) for x in parts]
+        return jnp.concatenate(wide, axis=1).reshape(tile, pairs)
+
+    ranks, codes = [], []
+    for device in here:
+        row = station - (device * station_dev).astype(jnp.float32)
+        hit = jnp.where((row >= 0.0) & (row < float(station_dev)), 1.0, 0.0)
+        ranks.append(jnp.where(hit > 0.0, count_before(hit), -1.0))
+        codes.append(((place + 1.0) * (1 << row_bits) + row) * (1 << shift_bits) + shift)
+
+    line = iota((SOURCES, halves * rows, 1), 1).reshape(tile, 1)
+    owner = iota((SOURCES, halves * rows, 1), 0).reshape(tile, 1)
+    block = jnp.zeros((tile, 1), jnp.int32)
+    for q in range(1, halves):
+        block = block + jnp.where(line >= q * rows, 1, 0)
+    line = line - block * rows
     comp = jnp.zeros((tile, 1), jnp.int32)
     for c in range(1, comps + 1):
         comp = comp + jnp.where(line >= c * capacity, 1, 0)
-    slot = line - comp * capacity
-    owner = jnp.zeros((tile, 1), jnp.int32)
-    for k in range(1, SOURCES):
-        owner = owner + jnp.where(block >= k * halves, 1, 0)
-    repeated = codes.astype(jnp.float32).reshape(blocks, 1, LANES)
-    repeated = jnp.broadcast_to(repeated, (blocks, rows, LANES)).reshape(tile, LANES)
-    chosen = (iota((tile, LANES), 1) == slot) & (comp < comps)
-    code = jnp.sum(jnp.where(chosen, repeated, 0.0), axis=1, keepdims=True).astype(jnp.int32)
-    shift_bits, row_bits = cfg["shift_bits"], cfg["row_bits"]
-    shift = code & ((1 << shift_bits) - 1)
+    slot = jnp.where(comp < comps, line - comp * capacity, -2).astype(jnp.float32)
+    code = jnp.sum(jnp.where(per_line(ranks) == slot, per_line(codes), 0.0), axis=1, keepdims=True)
+    code = code.astype(jnp.int32)
     row = lax.shift_right_logical(code, shift_bits) & ((1 << row_bits) - 1)
     tpl = lax.shift_right_logical(code, shift_bits + row_bits) - 1
-    goal = ((block - owner * halves) * comps + comp) * cfg["station_dev"] + row
-    return shift, jnp.where(tpl >= 0, goal, -1), jnp.where(tpl >= 0, owner * cfg["tpl_count"] + tpl, -1)
+    goal = (block * comps + comp) * station_dev + row
+    return (
+        code & ((1 << shift_bits) - 1),
+        jnp.where(tpl >= 0, goal, -1),
+        jnp.where(tpl >= 0, owner * tpl_count + tpl, -1),
+    )
 
 
 def cut_traces(cfg, shift, goal, waves):
@@ -235,9 +243,10 @@
     return table_ref[: 2 * LAGS, :], jnp.concatenate([high, low, high], axis=0)
 
 
-def trace_kernel(cfg, codes_ref, *refs):
+def trace_kernel(cfg, here_ref, lists_ref, *refs):
     waves_refs, (table_ref, edges_ref, kept_ref, sums_ref) = refs[:-4], refs[-4:]
-    shift, goal, column = tile_lines(cfg, codes_ref[...])
+    here = [here_ref[q] for q in range(cfg["halves"])]
+    shift, goal, column = tile_lines(cfg, here, lists_ref[...])
     waves = [ref[...].reshape(-1, ref.shape[2]) for ref in waves_refs]
     narrow = cut_traces(cfg, shift, goal, jnp.concatenate(waves, axis=0))
     kept_ref[:, 2 * cfg["length"] :] = levels_scale(cfg, narrow, edges_ref[...])
@@ -272,10 +281,11 @@
     lines = [pl.ds(t * tile, tile) for t in range(tiles)]
     halves = [pl.ds(q * 2 * LAGS, 2 * LAGS) for q in range(2)]
     forward = fetch(table_hbm, table_ref, halves[0])
+    part = tile // 2
     shapes, kept = [], []
     for t in range(tiles):
         shapes.append(fetch(shapes_hbm, shapes_ref, lines[t]))
-        kept.append(fetch(kept_hbm, kept_ref, lines[t]))
+        kept.append([fetch(kept_hbm, kept_ref, pl.ds(t * tile + k * part, part)) for k in range(2)])
         if t == 0:
             inverse = fetch(table_hbm, table_ref, halves[1])
             sums = fetch(sums_hbm, sums_ref)
@@ -283,18 +293,23 @@
     for t in range(tiles):
         shapes[t].wait()
         mine = shape_spectra(shapes_ref[lines[t], :], table_ref[: 2 * LAGS, :])
-        kept[t].wait()
-        theirs = kept_ref[lines[t], :]
-        spectra = [
-            (theirs[:, 2 * h * LAGS : (2 * h + 1) * LAGS], theirs[:, (2 * h + 1) * LAGS : (2 * h + 2) * LAGS])
-            for h in range(length // LAGS)
-        ]
         if t == 0:
             for copy in (inverse, sums):
                 copy.wait()
-        left = match_lines(mine, spectra, theirs[:, 2 * length :], tables_of(table_ref)[1])
         ends = pl.ds(t * groups, groups)
-        sent_ref[ends, :] = sum_lines(sums_ref[ends, :], left)
+        total = 0.0
+        for k in range(2):
+            kept[t][k].wait()
+            theirs = kept_ref[pl.ds(t * tile + k * part, part), :]
+            spectra = [
+                (theirs[:, 2 * h * LAGS : (2 * h + 1) * LAGS], theirs[:, (2 * h + 1) * LAGS : (2 * h + 2) * LAGS])
+                for h in range(length // LAGS)
+            ]
+            rows = slice(k * part, (k + 1) * part)
+            ours = [(real[rows], imag[rows]) for real, imag in mine]
+            left = match_lines(ours, spectra, theirs[:, 2 * length :], tables_of(table_ref)[1])
+            total = total + sum_lines(sums_ref[ends, rows], left)
+        sent_ref[ends, :] = total
 
 
 def stack_kernel(factor, parts_ref, stacks_ref, top_ref):
@@ -318,6 +333,7 @@
         halves=halves,
         station_dev=station_dev,
         tpl_count=tpl_count,
+        slot_count=slot_count,
         comps=comps,
         capacity=capacity,
         rows=rows,
@@ -339,6 +355,7 @@
     by_slot = templates.transpose(1, 2, 0, 3)
     waves = waveforms.transpose(1, 0, 2)
     half = lax.axis_index(HALF).reshape(1)
+    here = (lax.axis_index(AXES) + group * jnp.arange(halves, dtype=jnp.int32)) % devices
 
     def work(flops, size):
         return pl.CostEstimate(flops=flops, bytes_accessed=size, transcendentals=0)
@@ -353,25 +370,22 @@
         return pl.BlockSpec(shape, lambda i: (i, 0))
 
     traces = [waves] + [lax.ppermute(waves, HALF, [(0, 1), (1, 0)])] * (halves - 1)
-    codes, goal = pl.pallas_call(
+    lists = pl.pallas_call(
         functools.partial(list_kernel, cfg),
-        out_shape=[
-            jax.ShapeDtypeStruct((group * halves, LANES), jnp.int32),
-            jax.ShapeDtypeStruct((1, pairs), jnp.float32),
-        ],
-        in_specs=[pl.BlockSpec(memory_space=pltpu.SMEM), whole, whole],
-        out_specs=[whole, whole],
+        out_shape=jax.ShapeDtypeStruct((group, tpl_count, -(-slot_count // 128) * 128), jnp.int32),
+        in_specs=[whole, whole],
+        out_specs=whole,
         compiler_params=params,
         cost_estimate=work(1, 1),
         name="lists",
-    )(half, stations, moveouts)
-    codes = exchange(codes.reshape(group, halves, LANES), GROUP).reshape(group * halves, LANES)
+    )(stations, moveouts)
+    lists = exchange(lists, GROUP).reshape(group * tpl_count, lists.shape[2])
 
     pack_tiles = 4
     packed = pl.pallas_call(
         functools.partial(pack_kernel, cfg),
         out_shape=jax.ShapeDtypeStruct((lines, length), jnp.bfloat16),
-        in_specs=[whole, anywhere],
+        in_specs=[pl.BlockSpec(memory_space=pltpu.SMEM), whole, anywhere],
         out_specs=anywhere,
         scratch_shapes=[
             pltpu.VMEM(by_slot.shape, jnp.bfloat16),
@@ -383,8 +397,8 @@
         compiler_params=params,
         cost_estimate=work(5 * 10**9, 1),
         name="pack",
-    )(goal, by_slot)
-    codes, packed = lax.optimization_barrier((codes, packed))
+    )(half, stations, by_slot)
+    _, packed = lax.optimization_barrier((lists, packed))
     arrived = exchange(packed.reshape(group, halves * rows, length), GROUP).reshape(lines, length)
 
     kept, sums = pl.pallas_call(
@@ -394,14 +408,14 @@
             jax.ShapeDtypeStruct((lines, kept_len), jnp.float32),
             jax.ShapeDtypeStruct((group * tpl_count, tile), jnp.bfloat16),
         ],
-        in_specs=[tiled(SOURCES * halves, LANES)]
+        in_specs=[pl.BlockSpec(memory_space=pltpu.SMEM), tiled(sums_tile, lists.shape[1])]
         + [same(waves.shape)] * halves
         + [same((2 * LAGS, 2 * LAGS)), same(edges.shape)],
         out_specs=[tiled(tile, kept_len), tiled(sums_tile, tile)],
         compiler_params=params,
         cost_estimate=work(10**12, 1),
         name="traces",
-    )(codes, *traces, table, edges)
+    )(here, lists, *traces, table, edges)
     operands = (arrived, kept, sums, table)
     sent = pl.pallas_call(
         functools.partial(match_kernel, tiles),
@@ -409,7 +423,7 @@
         in_specs=[anywhere] * len(operands),
         out_specs=whole,
         scratch_shapes=[pltpu.VMEM(x.shape, x.dtype) for x in operands]
-        + [pltpu.SemaphoreType.DMA((3 + 2 * tiles,))],
+        + [pltpu.SemaphoreType.DMA((3 + 3 * tiles,))],
         compiler_params=pltpu.CompilerParams(vmem_limit_bytes=57 * MIB),
         name="match",
     )(*operands)

time: 91.4 us -> 91.2 us (level)
  waiting for transfers between devices: 21.4 us -> 20.1 us
    pallas_call x1, Pallas kernels: 14.2 us -> 15.2 us  [body(): pl.pallas_call(functools.partial(trace_kernel, cfg), grid=(tiles,), out_s...]
  transfers between devices with their start and end apart: 3 -> 3, of which waited for: 3 -> 3; matrix products, arithmetic and copies ran while one was open for 0% -> 1% of each run, Pallas kernels for 23% -> 24%
where the time goes in v1:
time: 91.2 us; the launch traced here: 90.7 us
  Pallas kernels  30.7 us (34%)
  blocking collectives  21.9 us (24%)
  waiting for transfers between devices  20.1 us (22%)
  starting transfers between devices  14.8 us (16%)
  local copies, waits for them, and re-layouts  1.47 us (2%)
  other arithmetic  1.14 us (1%)
    all_to_all x2, blocking collectives, exchange(): return lax.all_to_all(x, axes, split_axis=0, concat_axis=0, tiled=True)  21.9 us
    pallas_call x1, Pallas kernels, body(): pl.pallas_call(functools.partial(trace_kernel, cfg), grid=(tiles,), out_s...  15.2 us
    all_to_all x2, waiting for transfers between devices, exchange(): return lax.all_to_all(x, axes, split_axis=0, concat_axis=0, tiled=True)  12.8 us
    all_to_all x2, starting transfers between devices, exchange(): return lax.all_to_all(x, axes, split_axis=0, concat_axis=0, tiled=True)  10.6 us
    pallas_call x1, Pallas kernels, body(): pl.pallas_call(functools.partial(match_kernel, tiles), out_shape=jax.Shap...  8.61 us
    ppermute x1, waiting for transfers between devices, body(): lax.ppermute(waves, HALF, [(0, 1), (1, 0)])  7.36 us
    pallas_call x1, Pallas kernels, body(): pl.pallas_call(functools.partial(pack_kernel, cfg), out_shape=jax.ShapeDt...  4.93 us
    ppermute x1, starting transfers between devices, body(): lax.ppermute(waves, HALF, [(0, 1), (1, 0)])  4.1 us
  transfers between devices with their start and end apart: 3, of which 3 were waited for; matrix products, arithmetic and copies ran while one was open for 1% of the time, Pallas kernels for 24%

profile of v1, /device:TPU:0, one launch (start us, length us, event | category | flops | bytes accessed | tf_op | source)
XLA Modules:
  0.0 90.7 jit_solution(5858469256554018039)
XLA Ops:
  0.6 4.1 %collective-permute-start = (bf16[3,64,1664]{2,1,0:T(8,128)(2,1)}, bf16[3,64,1664]{2,1,0:T(8,128)(2,1)S(1)}, u32[]{:S(2)}, u32[]{:S(2)}) collective-permute-start(bf16[3,64,1664]{2,1,0:T(8,128)(2,1)} %bitcast.11), channel_id=1, source_target_pairs={{0,16},{16,0},{1,17},{17,1},{2,18},{18,2},{3,19},{19,3},{4,20},{20... | collective-permute-start | bytes 1916936 | tf_op jit(solution)/shard_map/ppermute | solution.py:372
  4.7 1.3 %lists.1 = s32[16,8,128]{2,1,0:T(8,128)} custom-call(s32[8,20]{1,0:T(8,128)} %stations_ref.3, s32[8,20]{1,0:T(8,128)} %moveouts_ref.1), custom_call_target="tpu_custom_call" | custom-call | flops 1 | bytes 1 | tf_op jit(solution)/shard_map/lists/pallas_call | solution.py:373
  6.1 4.8 %all-to-all-start = ((s32[16,8,128]{2,1,0:T(8,128)}), s32[16,8,128]{2,1,0:T(8,128)S(1)}, u32[]{:S(2)}, u32[]{:S(2)}) async-start(s32[16,8,128]{2,1,0:T(8,128)} %lists.1), calls=%async_computation | async-start | bytes 131072 | tf_op jit(solution)/shard_map/all_to_all | solution.py:364
  10.9 4.9 %pack.1 = bf16[1024,1024]{1,0:T(8,128)(2,1)} custom-call(s32[1]{0:T(128)} %bitcast.1.half_ref, s32[8,20]{1,0:T(8,128)} %stations_ref.3, bf16[20,3,8,1024]{3,2,1,0:T(8,128)(2,1)} %bitcast.10), custom_call_target="tpu_custom_call" | custom-call | flops 5000000000 | bytes 1 | tf_op jit(solution)/shard_map/pack/pallas_call | solution.py:385
  15.9 0.5 and_select_fusion.here_ref
  16.4 2.9 %all-to-all-done = s32[16,8,128]{2,1,0:T(8,128)S(1)} async-done(((s32[16,8,128]{2,1,0:T(8,128)}), s32[16,8,128]{2,1,0:T(8,128)S(1)}, u32[]{:S(2)}, u32[]{:S(2)}) %all-to-all-start) | async-done | bytes 65568 | tf_op jit(solution)/shard_map/all_to_all | solution.py:364
  19.3 0.0 copy-start
  19.3 0.6 copy-done
  19.9 5.8 %all-to-all-start.1 = ((bf16[16,64,1024]{2,1,0:T(8,128)(2,1)}), bf16[16,64,1024]{2,1,0:T(8,128)(2,1)}, u32[]{:S(2)}, u32[]{:S(2)}) async-start(bf16[16,64,1024]{2,1,0:T(8,128)(2,1)} %bitcast.7), calls=%async_computation.1 | async-start | bytes 4194304 | tf_op jit(solution)/shard_map/all_to_all | solution.py:364
  25.8 7.4 %collective-permute-done.refs_1_ = bf16[3,64,1664]{2,1,0:T(8,128)(2,1)S(1)} collective-permute-done((bf16[3,64,1664]{2,1,0:T(8,128)(2,1)}, bf16[3,64,1664]{2,1,0:T(8,128)(2,1)S(1)}, u32[]{:S(2)}, u32[]{:S(2)}) %collective-permute-start) | collective-permute-done | bytes 639008 | tf_op jit(solution)/shard_map/ppermute | solution.py:372
  33.1 0.0 copy-start.1
  33.1 0.9 copy-done.1
  34.0 15.2 %traces.1 = (f32[1024,2304]{1,0:T(8,128)}, bf16[128,512]{1,0:T(8,128)(2,1)}) custom-call(s32[2]{0:T(128)} %and_select_fusion.here_ref, s32[128,128]{1,0:T(8,128)} %bitcast.9, bf16[3,64,1664]{2,1,0:T(8,128)(2,1)} %bitcast.12, bf16[3,64,1664]{2,1,0:T(8,128)(2,1)} %copy-done.1, bf16[1024,512]{1,0:T(8,128)(2,1)} %constant.39.clone.refs_2_.table_hbm, ...), custom_call_target="tpu_custom_call" | custom-call | flops 999999995904 | bytes 1 | tf_op jit(solution)/shard_map/traces/pallas_call | solution.py:404
  49.1 9.8 %all-to-all-done.1 = bf16[16,64,1024]{2,1,0:T(8,128)(2,1)} async-done(((bf16[16,64,1024]{2,1,0:T(8,128)(2,1)}), bf16[16,64,1024]{2,1,0:T(8,128)(2,1)}, u32[]{:S(2)}, u32[]{:S(2)}) %all-to-all-start.1) | async-done | bytes 2097184 | tf_op jit(solution)/shard_map/all_to_all | solution.py:364
  59.0 8.6 %match.1 = f32[128,256]{1,0:T(8,128)} custom-call(bf16[1024,1024]{1,0:T(8,128)(2,1)} %bitcast.4.shapes_hbm, f32[1024,2304]{1,0:T(8,128)} %get-tuple-element.8.kept_hbm, bf16[128,512]{1,0:T(8,128)(2,1)} %get-tuple-element.9.sums_hbm, bf16[1024,512]{1,0:T(8,128)(2,1)} %constant.39.clone.refs_2_.table_hbm), custom_call_target="tpu_custom_call" | custom-call | tf_op jit(solution)/shard_map/match/pallas_call | solution.py:420
  67.6 10.6 %all_to_all.20.parts_ref = f32[16,8,256]{2,1,0:T(8,128)S(1)} all-to-all(f32[16,8,256]{2,1,0:T(8,128)} %bitcast.8), channel_id=1, replica_groups=mesh['half'=2,'tmpl'=4,'sta'=4] {'tmpl','sta'}, dimensions={0} | all-to-all | bytes 262144 | tf_op jit(solution)/shard_map/all_to_all | solution.py:364
  78.2 0.6 stack.1
  78.8 11.3 %all_to_all.21 = f32[32,1,256]{2,1,0:T(1,128)S(1)} all-to-all(f32[32,1,256]{2,1,0:T(1,128)S(1)} %get-tuple-element.11), channel_id=1, replica_groups=mesh['half'=2,'tmpl'=4,'sta'=4] {'half','tmpl','sta'}, dimensions={0} | all-to-all | bytes 65536 | tf_op jit(solution)/shard_map/all_to_all | solution.py:364
  90.1 0.6 reduce_max.9
Async XLA Ops:
  0.6 32.5 %collective-permute-start = (bf16[3,64,1664]{2,1,0:T(8,128)(2,1)}, bf16[3,64,1664]{2,1,0:T(8,128)(2,1)S(1)}, u32[]{:S(2)}, u32[]{:S(2)}) collective-permute-start(bf16[3,64,1664]{2,1,0:T(8,128)(2,1)} %bitcast.11), channel_id=1, source_target_pairs={{0,16},{16,0},{1,17},{17,1},{2,18},{18,2},{3,19},{19,3},{4,20},{20... | collective-permute-start | bytes 1916936 | tf_op jit(solution)/shard_map/ppermute | solution.py:372
  6.1 13.3 %all-to-all-start = ((s32[16,8,128]{2,1,0:T(8,128)}), s32[16,8,128]{2,1,0:T(8,128)S(1)}, u32[]{:S(2)}, u32[]{:S(2)}) async-start(s32[16,8,128]{2,1,0:T(8,128)} %lists.1), calls=%async_computation | async-start | bytes 131072 | tf_op jit(solution)/shard_map/all_to_all | solution.py:364
  19.3 0.6 copy-start
  19.9 39.0 %all-to-all-start.1 = ((bf16[16,64,1024]{2,1,0:T(8,128)(2,1)}), bf16[16,64,1024]{2,1,0:T(8,128)(2,1)}, u32[]{:S(2)}, u32[]{:S(2)}) async-start(bf16[16,64,1024]{2,1,0:T(8,128)(2,1)} %bitcast.7), calls=%async_computation.1 | async-start | bytes 4194304 | tf_op jit(solution)/shard_map/all_to_all | solution.py:364
  33.1 0.9 copy-start.1

commit v2 on v1

--- a/solution.py
+++ b/solution.py
@@ -99,8 +99,9 @@
     rank = jnp.sum(onehot * count_before(onehot), axis=0, keepdims=True)
     half = jnp.floor((device + 0.5) * (1.0 / group))
     away = jnp.where(half == half_ref[0].astype(jnp.float32), 0.0, 1.0)
-    goal = ((device - half * group) * halves + away) * rows + rank
-    goal = jnp.where(rank < float(cfg["capacity"]), goal, -float(group * halves * rows))
+    holder = device - half * group
+    capacity = cfg["capacity"]
+    base = jnp.where(rank < float(capacity), away * (cfg["comps"] * capacity) + rank, -1e6)
 
     comps, length = raw_ref.shape[1], raw_ref.shape[3]
     load.wait()
@@ -110,17 +111,35 @@
         spread_c = jnp.sqrt(jnp.mean(centred * centred, axis=-1, keepdims=True) + 1e-05)
         shapes_ref[c] = (centred * (1.0 / spread_c)).astype(jnp.bfloat16)
 
-    tiles = out_sems.shape[0]
-    tile = packed_ref.shape[0] // tiles
+    more, step_len = cfg["more"], 128
+    chunks = length // step_len - 1
+    tile = SOURCES * rows
     copies = []
-    for step in range(tiles):
-        line = iota((tile, pairs), 0).astype(jnp.float32) + float(step * tile)
-        total = jnp.zeros((tile, length), jnp.float32)
+    for step in range(group // SOURCES):
+        at = iota((tile, pairs), 0).astype(jnp.float32)
+        first = (holder - float(step * SOURCES)) * rows
+        low = jnp.zeros((tile, length), jnp.float32)
+        high = jnp.zeros((tile, chunks * step_len), jnp.float32)
+        lasts = [jnp.zeros((tile, step_len), jnp.float32) for _ in range(chunks)]
         for c in range(comps):
-            pick = jnp.where(line == goal + float(c * cfg["capacity"]), 1.0, 0.0).astype(jnp.bfloat16)
-            total = total + dot(pick, shapes_ref[c])
+            line = base + float(c * capacity)
+            extra = line - float(rows)
+            there = (extra >= 0.0) & (extra < float(more))
+            deep = jnp.floor((extra + 0.5) * (1.0 / chunks))
+            spot = jnp.where(there, extra - deep * chunks, -1.0)
+            shapes = shapes_ref[c]
+
+            def pick(ok, row):
+                return jnp.where(at == jnp.where(ok, first + row, -1.0), 1.0, 0.0).astype(jnp.bfloat16)
+
+            low = low + dot(pick((line >= 0.0) & (line < float(rows)), line), shapes)
+            high = high + dot(pick(there, extra), shapes[:, : chunks * step_len])
+            for m in range(chunks):
+                picked = pick(spot == float(m), float(more) + deep)
+                lasts[m] = lasts[m] + dot(picked, shapes[:, chunks * step_len :])
         part = pl.ds(step * tile, tile)
-        packed_ref[part, :] = total.astype(jnp.bfloat16)
+        packed_ref[part, :length] = low.astype(jnp.bfloat16)
+        packed_ref[part, length:] = (high + jnp.concatenate(lasts, axis=1)).astype(jnp.bfloat16)
         copies.append(pltpu.make_async_copy(packed_ref.at[part], packed_hbm.at[part], out_sems.at[step]))
         copies[-1].start()
     for copy in copies:
@@ -133,14 +152,14 @@
     tpl_count, slot_count = cfg["tpl_count"], cfg["slot_count"]
     lists = lists[:, :slot_count]
     pairs = tpl_count * slot_count
-    tile = SOURCES * halves * rows
+    tile = 2 * SOURCES * rows
     spread, place = entry_lanes(tpl_count, slot_count)
     station = as_lanes(lax.shift_right_logical(lists, shift_bits), spread, place, tpl_count)
     shift = as_lanes(lists & ((1 << shift_bits) - 1), spread, place, tpl_count)
 
-    def per_line(parts):
-        wide = [jnp.broadcast_to(x.reshape(SOURCES, 1, pairs), (SOURCES, rows, pairs)) for x in parts]
-        return jnp.concatenate(wide, axis=1).reshape(tile, pairs)
+    def per_line(x):
+        wide = jnp.broadcast_to(x.reshape(SOURCES, 1, pairs), (SOURCES, rows, pairs)).reshape(tile // 2, pairs)
+        return jnp.concatenate([wide, wide], axis=0)
 
     ranks, codes = [], []
     for device in here:
@@ -149,21 +168,22 @@
         ranks.append(jnp.where(hit > 0.0, count_before(hit), -1.0))
         codes.append(((place + 1.0) * (1 << row_bits) + row) * (1 << shift_bits) + shift)
 
-    line = iota((SOURCES, halves * rows, 1), 1).reshape(tile, 1)
-    owner = iota((SOURCES, halves * rows, 1), 0).reshape(tile, 1)
-    block = jnp.zeros((tile, 1), jnp.int32)
-    for q in range(1, halves):
-        block = block + jnp.where(line >= q * rows, 1, 0)
-    line = line - block * rows
-    comp = jnp.zeros((tile, 1), jnp.int32)
-    for c in range(1, comps + 1):
-        comp = comp + jnp.where(line >= c * capacity, 1, 0)
-    slot = jnp.where(comp < comps, line - comp * capacity, -2).astype(jnp.float32)
-    code = jnp.sum(jnp.where(per_line(ranks) == slot, per_line(codes), 0.0), axis=1, keepdims=True)
+    line = iota((SOURCES, rows, 1), 1).reshape(tile // 2, 1)
+    line = jnp.concatenate([line, line + rows], axis=0)
+    owner = iota((SOURCES, rows, 1), 0).reshape(tile // 2, 1)
+    owner = jnp.concatenate([owner, owner], axis=0)
+    panel = jnp.zeros((tile, 1), jnp.int32)
+    for m in range(1, halves * comps + 1):
+        panel = panel + jnp.where(line >= m * capacity, 1, 0)
+    slot = jnp.where(panel < halves * comps, line - panel * capacity, -2).astype(jnp.float32)
+    code = jnp.zeros((tile, 1), jnp.float32)
+    for q in range(halves):
+        mine = jnp.where((panel >= q * comps) & (panel < (q + 1) * comps), slot, -2.0)
+        code = code + jnp.sum(jnp.where(per_line(ranks[q]) == mine, per_line(codes[q]), 0.0), axis=1, keepdims=True)
     code = code.astype(jnp.int32)
     row = lax.shift_right_logical(code, shift_bits) & ((1 << row_bits) - 1)
     tpl = lax.shift_right_logical(code, shift_bits + row_bits) - 1
-    goal = (block * comps + comp) * station_dev + row
+    goal = panel * station_dev + row
     return (
         code & ((1 << shift_bits) - 1),
         jnp.where(tpl >= 0, goal, -1),
@@ -264,11 +284,32 @@
         before = here
 
 
-def match_kernel(tiles, shapes_hbm, kept_hbm, sums_hbm, table_hbm, sent_ref, *scratch):
+def line_pieces(cfg, packed):
+    rows, more, length = cfg["rows"], cfg["more"], cfg["length"]
+    tile = packed.shape[0]
+    chunks = length // 128 - 1
+    low, high = packed[:, :length], packed[:, length:]
+    number = iota((SOURCES, rows, 1), 1).reshape(tile, 1)
+    deep = jnp.zeros((tile, 1), jnp.int32)
+    for k in range(1, rows // chunks + 1):
+        deep = deep + jnp.where(number >= k * chunks, 1, 0)
+    source = iota((SOURCES, rows, 1), 0).reshape(tile, 1) * rows + more + deep
+    source = jnp.where(number < more, source, -1)
+    moved = dot(jnp.where(iota((tile, tile), 1) == source, 1.0, 0.0).astype(jnp.bfloat16), high)
+    last = jnp.zeros((tile, 128), jnp.float32)
+    for m in range(chunks):
+        last = last + jnp.where(number - deep * chunks == m, moved[:, m * 128 : (m + 1) * 128], 0.0)
+    high = jnp.concatenate([high, last.astype(jnp.bfloat16)], axis=1)
+    lines = jnp.concatenate([low, high], axis=0)
+    return lines
+
+
+def match_kernel(cfg, tiles, shapes_hbm, kept_hbm, sums_hbm, table_hbm, sent_ref, *scratch):
     shapes_ref, kept_ref, sums_ref, table_ref, sems = scratch
-    tile = shapes_ref.shape[0] // tiles
+    packed = shapes_ref.shape[0] // tiles
+    tile = kept_ref.shape[0] // tiles
     groups = sent_ref.shape[0] // tiles
-    length = shapes_ref.shape[1]
+    length = cfg["length"]
     copies = []
 
     def fetch(source, buffer, part=None):
@@ -278,7 +319,7 @@
         copies[-1].start()
         return copies[-1]
 
-    lines = [pl.ds(t * tile, tile) for t in range(tiles)]
+    lines = [pl.ds(t * packed, packed) for t in range(tiles)]
     halves = [pl.ds(q * 2 * LAGS, 2 * LAGS) for q in range(2)]
     forward = fetch(table_hbm, table_ref, halves[0])
     part = tile // 2
@@ -292,7 +333,7 @@
     forward.wait()
     for t in range(tiles):
         shapes[t].wait()
-        mine = shape_spectra(shapes_ref[lines[t], :], table_ref[: 2 * LAGS, :])
+        mine = shape_spectra(line_pieces(cfg, shapes_ref[lines[t], :]), table_ref[: 2 * LAGS, :])
         if t == 0:
             for copy in (inverse, sums):
                 copy.wait()
@@ -326,7 +367,12 @@
     seg_len = length + LAGS
     pairs = tpl_count * slot_count
     capacity = (2 * pairs + devices - 1) // devices
-    rows = -(-comps * capacity // 16) * 16
+    chunks = length // 128 - 1
+    total = halves * comps * capacity
+    rows = 16
+    while total - rows + max(0, -(-(total - rows) // chunks)) > rows:
+        rows += 16
+    more = max(0, total - rows)
     cfg = dict(
         devices=devices,
         group=group,
@@ -337,6 +383,7 @@
         comps=comps,
         capacity=capacity,
         rows=rows,
+        more=more,
         length=length,
         seg_len=seg_len,
         shift_bits=bits_of(samples - seg_len + 1),
@@ -345,8 +392,9 @@
     table = jnp.asarray(transform_table(LAGS))
     edges = jnp.asarray(edge_table(LAGS))
     tiles = group // SOURCES
-    tile = SOURCES * halves * rows
-    lines = group * halves * rows
+    tile = 2 * SOURCES * rows
+    lines = 2 * group * rows
+    width = length + chunks * 128
     sums_tile = SOURCES * tpl_count
     kept_len = 2 * length + LAGS
     whole = pl.BlockSpec(memory_space=pltpu.VMEM)
@@ -381,25 +429,24 @@
     )(stations, moveouts)
     lists = exchange(lists, GROUP).reshape(group * tpl_count, lists.shape[2])
 
-    pack_tiles = 4
     packed = pl.pallas_call(
         functools.partial(pack_kernel, cfg),
-        out_shape=jax.ShapeDtypeStruct((lines, length), jnp.bfloat16),
+        out_shape=jax.ShapeDtypeStruct((group * rows, width), jnp.bfloat16),
         in_specs=[pl.BlockSpec(memory_space=pltpu.SMEM), whole, anywhere],
         out_specs=anywhere,
         scratch_shapes=[
             pltpu.VMEM(by_slot.shape, jnp.bfloat16),
             pltpu.VMEM((comps, pairs, length), jnp.bfloat16),
-            pltpu.VMEM((lines, length), jnp.bfloat16),
+            pltpu.VMEM((group * rows, width), jnp.bfloat16),
             pltpu.SemaphoreType.DMA,
-            pltpu.SemaphoreType.DMA((pack_tiles,)),
+            pltpu.SemaphoreType.DMA((tiles,)),
         ],
         compiler_params=params,
         cost_estimate=work(5 * 10**9, 1),
         name="pack",
     )(half, stations, by_slot)
     _, packed = lax.optimization_barrier((lists, packed))
-    arrived = exchange(packed.reshape(group, halves * rows, length), GROUP).reshape(lines, length)
+    arrived = exchange(packed.reshape(group, rows, width), GROUP).reshape(group * rows, width)
 
     kept, sums = pl.pallas_call(
         functools.partial(trace_kernel, cfg),
@@ -418,7 +465,7 @@
     )(here, lists, *traces, table, edges)
     operands = (arrived, kept, sums, table)
     sent = pl.pallas_call(
-        functools.partial(match_kernel, tiles),
+        functools.partial(match_kernel, cfg, tiles),
         out_shape=jax.ShapeDtypeStruct((group * tpl_count, LAGS), jnp.float32),
         in_specs=[anywhere] * len(operands),
         out_specs=whole,

time: 91.2 us -> 89.4 us (0.980)
  waiting for transfers between devices: 20.1 us -> 17.2 us
  Pallas kernels: 30.7 us -> 32.3 us
    all_to_all x2, waiting for transfers between devices: 12.8 us -> 9.88 us  [exchange(): return lax.all_to_all(x, axes, split_axis=0, concat_axis=0, tiled=True)]
    pallas_call x1, Pallas kernels: 4.93 us -> 6.45 us  [body(): pl.pallas_call(functools.partial(pack_kernel, cfg), out_shape=jax.ShapeDt...]
  transfers between devices with their start and end apart: 3 -> 3, of which waited for: 3 -> 3; matrix products, arithmetic and copies ran while one was open for 1% -> 1% of each run, Pallas kernels for 24% -> 26%
where the time goes in v2:
time: 89.4 us; the launch traced here: 88.9 us
  Pallas kernels  32.3 us (36%)
  blocking collectives  21.3 us (24%)
  waiting for transfers between devices  17.2 us (19%)
  starting transfers between devices  14.7 us (16%)
  local copies, waits for them, and re-layouts  1.45 us (2%)
  other arithmetic  1.14 us (1%)
    all_to_all x2, blocking collectives, exchange(): return lax.all_to_all(x, axes, split_axis=0, concat_axis=0, tiled=True)  21.3 us
    pallas_call x1, Pallas kernels, body(): pl.pallas_call(functools.partial(trace_kernel, cfg), grid=(tiles,), out_s...  15.1 us
    all_to_all x2, starting transfers between devices, exchange(): return lax.all_to_all(x, axes, split_axis=0, concat_axis=0, tiled=True)  10.6 us
    all_to_all x2, waiting for transfers between devices, exchange(): return lax.all_to_all(x, axes, split_axis=0, concat_axis=0, tiled=True)  9.88 us
    pallas_call x1, Pallas kernels, body(): pl.pallas_call(functools.partial(match_kernel, cfg, tiles), out_shape=jax...  8.8 us
    ppermute x1, waiting for transfers between devices, body(): lax.ppermute(waves, HALF, [(0, 1), (1, 0)])  7.36 us
    pallas_call x1, Pallas kernels, body(): pl.pallas_call(functools.partial(pack_kernel, cfg), out_shape=jax.ShapeDt...  6.45 us
    ppermute x1, starting transfers between devices, body(): lax.ppermute(waves, HALF, [(0, 1), (1, 0)])  4.1 us
  transfers between devices with their start and end apart: 3, of which 3 were waited for; matrix products, arithmetic and copies ran while one was open for 1% of the time, Pallas kernels for 26%

profile of v2, /device:TPU:0, one launch (start us, length us, event | category | flops | bytes accessed | tf_op | source)
XLA Modules:
  0.0 88.9 jit_solution(13656633737654575949)
XLA Ops:
  0.6 4.1 %collective-permute-start = (bf16[3,64,1664]{2,1,0:T(8,128)(2,1)}, bf16[3,64,1664]{2,1,0:T(8,128)(2,1)S(1)}, u32[]{:S(2)}, u32[]{:S(2)}) collective-permute-start(bf16[3,64,1664]{2,1,0:T(8,128)(2,1)} %bitcast.11), channel_id=1, source_target_pairs={{0,16},{16,0},{1,17},{17,1},{2,18},{18,2},{3,19},{19,3},{4,20},{20... | collective-permute-start | bytes 1916936 | tf_op jit(solution)/shard_map/ppermute | solution.py:420
  4.7 1.3 %lists.1 = s32[16,8,128]{2,1,0:T(8,128)} custom-call(s32[8,20]{1,0:T(8,128)} %stations_ref.3, s32[8,20]{1,0:T(8,128)} %moveouts_ref.1), custom_call_target="tpu_custom_call" | custom-call | flops 1 | bytes 1 | tf_op jit(solution)/shard_map/lists/pallas_call | solution.py:421
  6.1 4.8 %all-to-all-start = ((s32[16,8,128]{2,1,0:T(8,128)}), s32[16,8,128]{2,1,0:T(8,128)S(1)}, u32[]{:S(2)}, u32[]{:S(2)}) async-start(s32[16,8,128]{2,1,0:T(8,128)} %lists.1), calls=%async_computation | async-start | bytes 131072 | tf_op jit(solution)/shard_map/all_to_all | solution.py:412
  10.9 6.5 %pack.1 = bf16[512,1920]{1,0:T(8,128)(2,1)} custom-call(s32[1]{0:T(128)} %bitcast.1.half_ref, s32[8,20]{1,0:T(8,128)} %stations_ref.3, bf16[20,3,8,1024]{3,2,1,0:T(8,128)(2,1)} %bitcast.10), custom_call_target="tpu_custom_call" | custom-call | flops 5000000000 | bytes 1 | tf_op jit(solution)/shard_map/pack/pallas_call | solution.py:432
  17.4 0.5 and_select_fusion.here_ref
  17.9 1.4 %all-to-all-done = s32[16,8,128]{2,1,0:T(8,128)S(1)} async-done(((s32[16,8,128]{2,1,0:T(8,128)}), s32[16,8,128]{2,1,0:T(8,128)S(1)}, u32[]{:S(2)}, u32[]{:S(2)}) %all-to-all-start) | async-done | bytes 65568 | tf_op jit(solution)/shard_map/all_to_all | solution.py:412
  19.3 0.0 copy-start
  19.3 0.6 copy-done
  20.0 5.8 %all-to-all-start.1 = ((bf16[16,32,1920]{2,1,0:T(8,128)(2,1)}), bf16[16,32,1920]{2,1,0:T(8,128)(2,1)}, u32[]{:S(2)}, u32[]{:S(2)}) async-start(bf16[16,32,1920]{2,1,0:T(8,128)(2,1)} %bitcast.7), calls=%async_computation.1 | async-start | bytes 3932160 | tf_op jit(solution)/shard_map/all_to_all | solution.py:412
  25.8 7.4 %collective-permute-done.refs_1_ = bf16[3,64,1664]{2,1,0:T(8,128)(2,1)S(1)} collective-permute-done((bf16[3,64,1664]{2,1,0:T(8,128)(2,1)}, bf16[3,64,1664]{2,1,0:T(8,128)(2,1)S(1)}, u32[]{:S(2)}, u32[]{:S(2)}) %collective-permute-start) | collective-permute-done | bytes 639008 | tf_op jit(solution)/shard_map/ppermute | solution.py:420
  33.1 0.0 copy-start.1
  33.1 0.8 copy-done.1
  34.0 15.1 %traces.1 = (f32[1024,2304]{1,0:T(8,128)}, bf16[128,512]{1,0:T(8,128)(2,1)}) custom-call(s32[2]{0:T(128)} %and_select_fusion.here_ref, s32[128,128]{1,0:T(8,128)} %bitcast.9, bf16[3,64,1664]{2,1,0:T(8,128)(2,1)} %bitcast.12, bf16[3,64,1664]{2,1,0:T(8,128)(2,1)} %copy-done.1, bf16[1024,512]{1,0:T(8,128)(2,1)} %constant.39.clone.refs_2_.table_hbm, ...), custom_call_target="tpu_custom_call" | custom-call | flops 999999995904 | bytes 1 | tf_op jit(solution)/shard_map/traces/pallas_call | solution.py:451
  49.1 8.5 %all-to-all-done.1 = bf16[16,32,1920]{2,1,0:T(8,128)(2,1)} async-done(((bf16[16,32,1920]{2,1,0:T(8,128)(2,1)}), bf16[16,32,1920]{2,1,0:T(8,128)(2,1)}, u32[]{:S(2)}, u32[]{:S(2)}) %all-to-all-start.1) | async-done | bytes 1966112 | tf_op jit(solution)/shard_map/all_to_all | solution.py:412
  57.6 8.8 %match.1 = f32[128,256]{1,0:T(8,128)} custom-call(bf16[512,1920]{1,0:T(8,128)(2,1)} %bitcast.4.shapes_hbm, f32[1024,2304]{1,0:T(8,128)} %get-tuple-element.8.kept_hbm, bf16[128,512]{1,0:T(8,128)(2,1)} %get-tuple-element.9.sums_hbm, bf16[1024,512]{1,0:T(8,128)(2,1)} %constant.39.clone.refs_2_.table_hbm), custom_call_target="tpu_custom_call" | custom-call | tf_op jit(solution)/shard_map/match/pallas_call | solution.py:467
  66.4 10.1 %all_to_all.20.parts_ref = f32[16,8,256]{2,1,0:T(8,128)S(1)} all-to-all(f32[16,8,256]{2,1,0:T(8,128)} %bitcast.8), channel_id=1, replica_groups=mesh['half'=2,'tmpl'=4,'sta'=4] {'tmpl','sta'}, dimensions={0} | all-to-all | bytes 262144 | tf_op jit(solution)/shard_map/all_to_all | solution.py:412
  76.4 0.6 stack.1
  77.0 11.3 %all_to_all.21 = f32[32,1,256]{2,1,0:T(1,128)S(1)} all-to-all(f32[32,1,256]{2,1,0:T(1,128)S(1)} %get-tuple-element.11), channel_id=1, replica_groups=mesh['half'=2,'tmpl'=4,'sta'=4] {'half','tmpl','sta'}, dimensions={0} | all-to-all | bytes 65536 | tf_op jit(solution)/shard_map/all_to_all | solution.py:412
  88.3 0.6 reduce_max.9
Async XLA Ops:
  0.6 32.5 %collective-permute-start = (bf16[3,64,1664]{2,1,0:T(8,128)(2,1)}, bf16[3,64,1664]{2,1,0:T(8,128)(2,1)S(1)}, u32[]{:S(2)}, u32[]{:S(2)}) collective-permute-start(bf16[3,64,1664]{2,1,0:T(8,128)(2,1)} %bitcast.11), channel_id=1, source_target_pairs={{0,16},{16,0},{1,17},{17,1},{2,18},{18,2},{3,19},{19,3},{4,20},{20... | collective-permute-start | bytes 1916936 | tf_op jit(solution)/shard_map/ppermute | solution.py:420
  6.1 13.3 %all-to-all-start = ((s32[16,8,128]{2,1,0:T(8,128)}), s32[16,8,128]{2,1,0:T(8,128)S(1)}, u32[]{:S(2)}, u32[]{:S(2)}) async-start(s32[16,8,128]{2,1,0:T(8,128)} %lists.1), calls=%async_computation | async-start | bytes 131072 | tf_op jit(solution)/shard_map/all_to_all | solution.py:412
  19.3 0.6 copy-start
  20.0 37.6 %all-to-all-start.1 = ((bf16[16,32,1920]{2,1,0:T(8,128)(2,1)}), bf16[16,32,1920]{2,1,0:T(8,128)(2,1)}, u32[]{:S(2)}, u32[]{:S(2)}) async-start(bf16[16,32,1920]{2,1,0:T(8,128)(2,1)} %bitcast.7), calls=%async_computation.1 | async-start | bytes 3932160 | tf_op jit(solution)/shard_map/all_to_all | solution.py:412
  33.1 0.8 copy-start.1

commit v3 on v2

--- a/solution.py
+++ b/solution.py
@@ -12,8 +12,9 @@
 
 LAGS = 256
 HALF = "half"
-GROUP = ("tmpl", "sta")
-AXES = (HALF,) + GROUP
+DEEP = "deep"
+AXES = (HALF, DEEP, "wide", "sta")
+GROUP = ("wide", "sta", DEEP)
 SOURCES = 8
 MIB = 1024 * 1024
 
@@ -100,6 +101,9 @@
     half = jnp.floor((device + 0.5) * (1.0 / group))
     away = jnp.where(half == half_ref[0].astype(jnp.float32), 0.0, 1.0)
     holder = device - half * group
+    inner = group // cfg["deep"]
+    part_of = jnp.floor((holder + 0.5) * (1.0 / inner))
+    holder = (holder - part_of * inner) * cfg["deep"] + part_of
     capacity = cfg["capacity"]
     base = jnp.where(rank < float(capacity), away * (cfg["comps"] * capacity) + rank, -1e6)
 
@@ -265,7 +269,10 @@
 
 def trace_kernel(cfg, here_ref, lists_ref, *refs):
     waves_refs, (table_ref, edges_ref, kept_ref, sums_ref) = refs[:-4], refs[-4:]
-    here = [here_ref[q] for q in range(cfg["halves"])]
+    here = [here_ref[0]]
+    for _ in range(1, cfg["halves"]):
+        other = here[-1] + cfg["group"]
+        here.append(jnp.where(other >= cfg["devices"], other - cfg["devices"], other))
     shift, goal, column = tile_lines(cfg, here, lists_ref[...])
     waves = [ref[...].reshape(-1, ref.shape[2]) for ref in waves_refs]
     narrow = cut_traces(cfg, shift, goal, jnp.concatenate(waves, axis=0))
@@ -377,6 +384,7 @@
         devices=devices,
         group=group,
         halves=halves,
+        deep=lax.axis_size(DEEP),
         station_dev=station_dev,
         tpl_count=tpl_count,
         slot_count=slot_count,
@@ -403,7 +411,7 @@
     by_slot = templates.transpose(1, 2, 0, 3)
     waves = waveforms.transpose(1, 0, 2)
     half = lax.axis_index(HALF).reshape(1)
-    here = (lax.axis_index(AXES) + group * jnp.arange(halves, dtype=jnp.int32)) % devices
+    here = lax.axis_index(AXES).reshape(1)
 
     def work(flops, size):
         return pl.CostEstimate(flops=flops, bytes_accessed=size, transcendentals=0)
@@ -491,9 +499,10 @@
 
 
 def solution(mesh):
-    slow, fast = (mesh.shape[name] for name in GROUP)
+    slow, fast = mesh.devices.shape
     halves = 2 if slow % 2 == 0 else 1
-    split = jax.sharding.Mesh(mesh.devices.reshape(halves, slow // halves, fast), AXES)
+    deep = 2 if slow // halves % 2 == 0 else 1
+    split = jax.sharding.Mesh(mesh.devices.reshape(halves, deep, slow // halves // deep, fast), AXES)
     placed = (
         P(AXES, None, None),
         P(AXES, None, None, None),

time: 89.4 us -> 87.4 us (0.978)
  transfers between devices with their start and end apart: 3 -> 3, of which waited for: 3 -> 3; matrix products, arithmetic and copies ran while one was open for 1% -> 0% of each run, Pallas kernels for 26% -> 26%
where the time goes in v3:
time: 87.4 us; the launch traced here: 86.9 us
  Pallas kernels  32.3 us (37%)
  blocking collectives  20.6 us (24%)
  waiting for transfers between devices  16.5 us (19%)
  starting transfers between devices  14.7 us (17%)
  local copies, waits for them, and re-layouts  1.45 us (2%)
    all_to_all x2, blocking collectives, exchange(): return lax.all_to_all(x, axes, split_axis=0, concat_axis=0, tiled=True)  20.6 us
    pallas_call x1, Pallas kernels, body(): pl.pallas_call(functools.partial(trace_kernel, cfg), grid=(tiles,), out_s...  15.1 us
    all_to_all x2, starting transfers between devices, exchange(): return lax.all_to_all(x, axes, split_axis=0, concat_axis=0, tiled=True)  10.6 us
    all_to_all x2, waiting for transfers between devices, exchange(): return lax.all_to_all(x, axes, split_axis=0, concat_axis=0, tiled=True)  9.11 us
    pallas_call x1, Pallas kernels, body(): pl.pallas_call(functools.partial(match_kernel, cfg, tiles), out_shape=jax...  8.8 us
    ppermute x1, waiting for transfers between devices, body(): lax.ppermute(waves, HALF, [(0, 1), (1, 0)])  7.4 us
    pallas_call x1, Pallas kernels, body(): pl.pallas_call(functools.partial(pack_kernel, cfg), out_shape=jax.ShapeDt...  6.45 us
    ppermute x1, starting transfers between devices, body(): lax.ppermute(waves, HALF, [(0, 1), (1, 0)])  4.1 us
  transfers between devices with their start and end apart: 3, of which 3 were waited for; matrix products, arithmetic and copies ran while one was open for 0% of the time, Pallas kernels for 26%

profile of v3, /device:TPU:0, one launch (start us, length us, event | category | flops | bytes accessed | tf_op | source)
XLA Modules:
  0.0 86.9 jit_solution(7191119637953551102)
XLA Ops:
  0.6 4.1 %collective-permute-start = (bf16[3,64,1664]{2,1,0:T(8,128)(2,1)}, bf16[3,64,1664]{2,1,0:T(8,128)(2,1)S(1)}, u32[]{:S(2)}, u32[]{:S(2)}) collective-permute-start(bf16[3,64,1664]{2,1,0:T(8,128)(2,1)} %bitcast.12), channel_id=1, source_target_pairs={{0,16},{16,0},{1,17},{17,1},{2,18},{18,2},{3,19},{19,3},{4,20},{20... | collective-permute-start | bytes 1916936 | tf_op jit(solution)/shard_map/ppermute | solution.py:428
  4.7 1.3 %lists.1 = s32[16,8,128]{2,1,0:T(8,128)} custom-call(s32[8,20]{1,0:T(8,128)} %stations_ref.3, s32[8,20]{1,0:T(8,128)} %moveouts_ref.1), custom_call_target="tpu_custom_call" | custom-call | flops 1 | bytes 1 | tf_op jit(solution)/shard_map/lists/pallas_call | solution.py:429
  6.1 4.8 %all-to-all-start = ((s32[16,8,128]{2,1,0:T(8,128)}), s32[16,8,128]{2,1,0:T(8,128)S(1)}, u32[]{:S(2)}, u32[]{:S(2)}) async-start(s32[16,8,128]{2,1,0:T(8,128)} %lists.1), calls=%async_computation | async-start | bytes 131072 | tf_op jit(solution)/shard_map/all_to_all | solution.py:420
  10.9 6.5 %pack.1 = bf16[512,1920]{1,0:T(8,128)(2,1)} custom-call(s32[1]{0:T(128)} %bitcast.1.half_ref, s32[8,20]{1,0:T(8,128)} %stations_ref.3, bf16[20,3,8,1024]{3,2,1,0:T(8,128)(2,1)} %bitcast.11), custom_call_target="tpu_custom_call" | custom-call | flops 5000000000 | bytes 1 | tf_op jit(solution)/shard_map/pack/pallas_call | solution.py:440
  17.4 1.9 %all-to-all-done = s32[16,8,128]{2,1,0:T(8,128)S(1)} async-done(((s32[16,8,128]{2,1,0:T(8,128)}), s32[16,8,128]{2,1,0:T(8,128)S(1)}, u32[]{:S(2)}, u32[]{:S(2)}) %all-to-all-start) | async-done | bytes 65568 | tf_op jit(solution)/shard_map/all_to_all | solution.py:420
  19.3 0.0 copy-start
  19.3 0.6 copy-done
  20.0 5.8 %all-to-all-start.1 = ((bf16[16,32,1920]{2,1,0:T(8,128)(2,1)}), bf16[16,32,1920]{2,1,0:T(8,128)(2,1)}, u32[]{:S(2)}, u32[]{:S(2)}) async-start(bf16[16,32,1920]{2,1,0:T(8,128)(2,1)} %bitcast.8), calls=%async_computation.1 | async-start | bytes 3932160 | tf_op jit(solution)/shard_map/all_to_all | solution.py:420
  25.7 7.4 %collective-permute-done.refs_1_ = bf16[3,64,1664]{2,1,0:T(8,128)(2,1)S(1)} collective-permute-done((bf16[3,64,1664]{2,1,0:T(8,128)(2,1)}, bf16[3,64,1664]{2,1,0:T(8,128)(2,1)S(1)}, u32[]{:S(2)}, u32[]{:S(2)}) %collective-permute-start) | collective-permute-done | bytes 639008 | tf_op jit(solution)/shard_map/ppermute | solution.py:428
  33.1 0.0 copy-start.1
  33.1 0.8 copy-done.1
  34.0 15.1 %traces.1 = (f32[1024,2304]{1,0:T(8,128)}, bf16[128,512]{1,0:T(8,128)(2,1)}) custom-call(s32[1]{0:T(128)} %bitcast.5.here_ref, s32[128,128]{1,0:T(8,128)} %bitcast.10, bf16[3,64,1664]{2,1,0:T(8,128)(2,1)} %bitcast.13, bf16[3,64,1664]{2,1,0:T(8,128)(2,1)} %copy-done.1, bf16[1024,512]{1,0:T(8,128)(2,1)} %constant.28.clone.refs_2_.table_hbm, ...), custom_call_target="tpu_custom_call" | custom-call | flops 999999995904 | bytes 1 | tf_op jit(solution)/shard_map/traces/pallas_call | solution.py:459
  49.1 7.2 %all-to-all-done.1 = bf16[16,32,1920]{2,1,0:T(8,128)(2,1)} async-done(((bf16[16,32,1920]{2,1,0:T(8,128)(2,1)}), bf16[16,32,1920]{2,1,0:T(8,128)(2,1)}, u32[]{:S(2)}, u32[]{:S(2)}) %all-to-all-start.1) | async-done | bytes 1966112 | tf_op jit(solution)/shard_map/all_to_all | solution.py:420
  56.3 8.8 %match.1 = f32[128,256]{1,0:T(8,128)} custom-call(bf16[512,1920]{1,0:T(8,128)(2,1)} %bitcast.4.shapes_hbm, f32[1024,2304]{1,0:T(8,128)} %get-tuple-element.8.kept_hbm, bf16[128,512]{1,0:T(8,128)(2,1)} %get-tuple-element.9.sums_hbm, bf16[1024,512]{1,0:T(8,128)(2,1)} %constant.28.clone.refs_2_.table_hbm), custom_call_target="tpu_custom_call" | custom-call | tf_op jit(solution)/shard_map/match/pallas_call | solution.py:475
  65.1 9.2 %all_to_all.20.parts_ref = f32[16,8,256]{2,1,0:T(8,128)S(1)} all-to-all(f32[16,8,256]{2,1,0:T(8,128)} %bitcast.9), channel_id=1, replica_groups=mesh['half'=2,'deep'=2,'wide'=2,'sta'=4] {'wide','sta','deep'}, dimensions={0} | all-to-all | bytes 262144 | tf_op jit(solution)/shard_map/all_to_all | solution.py:420
  74.3 0.6 stack.1
  74.9 11.4 %all_to_all.21 = f32[32,1,256]{2,1,0:T(1,128)S(1)} all-to-all(f32[32,1,256]{2,1,0:T(1,128)S(1)} %get-tuple-element.11), channel_id=1, replica_groups=mesh['half'=2,'deep'=2,'wide'=2,'sta'=4] {'half','deep','wide','sta'}, dimensions={0} | all-to-all | bytes 65536 | tf_op jit(solution)/shard_map/all_to_all | solution.py:420
  86.3 0.6 reduce_max.9
Async XLA Ops:
  0.6 32.5 %collective-permute-start = (bf16[3,64,1664]{2,1,0:T(8,128)(2,1)}, bf16[3,64,1664]{2,1,0:T(8,128)(2,1)S(1)}, u32[]{:S(2)}, u32[]{:S(2)}) collective-permute-start(bf16[3,64,1664]{2,1,0:T(8,128)(2,1)} %bitcast.12), channel_id=1, source_target_pairs={{0,16},{16,0},{1,17},{17,1},{2,18},{18,2},{3,19},{19,3},{4,20},{20... | collective-permute-start | bytes 1916936 | tf_op jit(solution)/shard_map/ppermute | solution.py:428
  6.1 13.3 %all-to-all-start = ((s32[16,8,128]{2,1,0:T(8,128)}), s32[16,8,128]{2,1,0:T(8,128)S(1)}, u32[]{:S(2)}, u32[]{:S(2)}) async-start(s32[16,8,128]{2,1,0:T(8,128)} %lists.1), calls=%async_computation | async-start | bytes 131072 | tf_op jit(solution)/shard_map/all_to_all | solution.py:420
  19.3 0.6 copy-start
  20.0 36.3 %all-to-all-start.1 = ((bf16[16,32,1920]{2,1,0:T(8,128)(2,1)}), bf16[16,32,1920]{2,1,0:T(8,128)(2,1)}, u32[]{:S(2)}, u32[]{:S(2)}) async-start(bf16[16,32,1920]{2,1,0:T(8,128)(2,1)} %bitcast.8), calls=%async_computation.1 | async-start | bytes 3932160 | tf_op jit(solution)/shard_map/all_to_all | solution.py:420
  33.1 0.8 copy-start.1

commit v4 on v3

--- a/solution.py
+++ b/solution.py
@@ -13,8 +13,9 @@
 LAGS = 256
 HALF = "half"
 DEEP = "deep"
-AXES = (HALF, DEEP, "wide", "sta")
-GROUP = ("wide", "sta", DEEP)
+PARTS = (DEEP, "wide", "sta", "core")
+AXES = (HALF,) + PARTS
+GROUP = PARTS[::-1]
 SOURCES = 8
 MIB = 1024 * 1024
 
@@ -101,9 +102,12 @@
     half = jnp.floor((device + 0.5) * (1.0 / group))
     away = jnp.where(half == half_ref[0].astype(jnp.float32), 0.0, 1.0)
     holder = device - half * group
-    inner = group // cfg["deep"]
-    part_of = jnp.floor((holder + 0.5) * (1.0 / inner))
-    holder = (holder - part_of * inner) * cfg["deep"] + part_of
+    number = jnp.zeros_like(holder)
+    for size in cfg["parts"][::-1]:
+        rest = jnp.floor((holder + 0.5) * (1.0 / size))
+        number = number * size + (holder - rest * size)
+        holder = rest
+    holder = number
     capacity = cfg["capacity"]
     base = jnp.where(rank < float(capacity), away * (cfg["comps"] * capacity) + rank, -1e6)
 
@@ -384,7 +388,7 @@
         devices=devices,
         group=group,
         halves=halves,
-        deep=lax.axis_size(DEEP),
+        parts=[lax.axis_size(name) for name in PARTS],
         station_dev=station_dev,
         tpl_count=tpl_count,
         slot_count=slot_count,
@@ -502,7 +506,9 @@
     slow, fast = mesh.devices.shape
     halves = 2 if slow % 2 == 0 else 1
     deep = 2 if slow // halves % 2 == 0 else 1
-    split = jax.sharding.Mesh(mesh.devices.reshape(halves, deep, slow // halves // deep, fast), AXES)
+    cores = 2 if fast % 2 == 0 else 1
+    shape = (halves, deep, slow // halves // deep, fast // cores, cores)
+    split = jax.sharding.Mesh(mesh.devices.reshape(shape), AXES)
     placed = (
         P(AXES, None, None),
         P(AXES, None, None, None),

time: 87.4 us -> 87.5 us (level)
  no operation moved by 1% of the time
where the time goes in v4:
time: 87.5 us; the launch traced here: 87 us
  Pallas kernels  32.3 us (37%)
  blocking collectives  20.2 us (23%)
  waiting for transfers between devices  17 us (19%)
  starting transfers between devices  14.7 us (17%)
  local copies, waits for them, and re-layouts  1.45 us (2%)
    all_to_all x2, blocking collectives, exchange(): return lax.all_to_all(x, axes, split_axis=0, concat_axis=0, tiled=True)  20.2 us
    pallas_call x1, Pallas kernels, body(): pl.pallas_call(functools.partial(trace_kernel, cfg), grid=(tiles,), out_s...  15.1 us
    all_to_all x2, starting transfers between devices, exchange(): return lax.all_to_all(x, axes, split_axis=0, concat_axis=0, tiled=True)  10.6 us
    all_to_all x2, waiting for transfers between devices, exchange(): return lax.all_to_all(x, axes, split_axis=0, concat_axis=0, tiled=True)  9.6 us
    pallas_call x1, Pallas kernels, body(): pl.pallas_call(functools.partial(match_kernel, cfg, tiles), out_shape=jax...  8.8 us
    ppermute x1, waiting for transfers between devices, body(): lax.ppermute(waves, HALF, [(0, 1), (1, 0)])  7.36 us
    pallas_call x1, Pallas kernels, body(): pl.pallas_call(functools.partial(pack_kernel, cfg), out_shape=jax.ShapeDt...  6.46 us
    ppermute x1, starting transfers between devices, body(): lax.ppermute(waves, HALF, [(0, 1), (1, 0)])  4.1 us
  transfers between devices with their start and end apart: 3, of which 3 were waited for; matrix products, arithmetic and copies ran while one was open for 0% of the time, Pallas kernels for 26%

profile of v4, /device:TPU:0, one launch (start us, length us, event | category | flops | bytes accessed | tf_op | source)
XLA Modules:
  0.0 87.0 jit_solution(15440807632868946230)
XLA Ops:
  0.6 4.1 %collective-permute-start = (bf16[3,64,1664]{2,1,0:T(8,128)(2,1)}, bf16[3,64,1664]{2,1,0:T(8,128)(2,1)S(1)}, u32[]{:S(2)}, u32[]{:S(2)}) collective-permute-start(bf16[3,64,1664]{2,1,0:T(8,128)(2,1)} %bitcast.12), channel_id=1, source_target_pairs={{0,16},{16,0},{1,17},{17,1},{2,18},{18,2},{3,19},{19,3},{4,20},{20... | collective-permute-start | bytes 1916936 | tf_op jit(solution)/shard_map/ppermute | solution.py:432
  4.7 1.3 %lists.1 = s32[16,8,128]{2,1,0:T(8,128)} custom-call(s32[8,20]{1,0:T(8,128)} %stations_ref.3, s32[8,20]{1,0:T(8,128)} %moveouts_ref.1), custom_call_target="tpu_custom_call" | custom-call | flops 1 | bytes 1 | tf_op jit(solution)/shard_map/lists/pallas_call | solution.py:433
  6.1 4.8 %all-to-all-start = ((s32[16,8,128]{2,1,0:T(8,128)}), s32[16,8,128]{2,1,0:T(8,128)S(1)}, u32[]{:S(2)}, u32[]{:S(2)}) async-start(s32[16,8,128]{2,1,0:T(8,128)} %lists.1), calls=%async_computation | async-start | bytes 131072 | tf_op jit(solution)/shard_map/all_to_all | solution.py:424
  10.9 6.5 %pack.1 = bf16[512,1920]{1,0:T(8,128)(2,1)} custom-call(s32[1]{0:T(128)} %bitcast.1.half_ref, s32[8,20]{1,0:T(8,128)} %stations_ref.3, bf16[20,3,8,1024]{3,2,1,0:T(8,128)(2,1)} %bitcast.11), custom_call_target="tpu_custom_call" | custom-call | flops 5000000000 | bytes 1 | tf_op jit(solution)/shard_map/pack/pallas_call | solution.py:444
  17.4 1.9 %all-to-all-done = s32[16,8,128]{2,1,0:T(8,128)S(1)} async-done(((s32[16,8,128]{2,1,0:T(8,128)}), s32[16,8,128]{2,1,0:T(8,128)S(1)}, u32[]{:S(2)}, u32[]{:S(2)}) %all-to-all-start) | async-done | bytes 65568 | tf_op jit(solution)/shard_map/all_to_all | solution.py:424
  19.3 0.0 copy-start
  19.3 0.6 copy-done
  20.0 5.8 %all-to-all-start.1 = ((bf16[16,32,1920]{2,1,0:T(8,128)(2,1)}), bf16[16,32,1920]{2,1,0:T(8,128)(2,1)}, u32[]{:S(2)}, u32[]{:S(2)}) async-start(bf16[16,32,1920]{2,1,0:T(8,128)(2,1)} %bitcast.8), calls=%async_computation.1 | async-start | bytes 3932160 | tf_op jit(solution)/shard_map/all_to_all | solution.py:424
  25.8 7.4 %collective-permute-done.refs_1_ = bf16[3,64,1664]{2,1,0:T(8,128)(2,1)S(1)} collective-permute-done((bf16[3,64,1664]{2,1,0:T(8,128)(2,1)}, bf16[3,64,1664]{2,1,0:T(8,128)(2,1)S(1)}, u32[]{:S(2)}, u32[]{:S(2)}) %collective-permute-start) | collective-permute-done | bytes 639008 | tf_op jit(solution)/shard_map/ppermute | solution.py:432
  33.1 0.0 copy-start.1
  33.1 0.8 copy-done.1
  34.0 15.1 %traces.1 = (f32[1024,2304]{1,0:T(8,128)}, bf16[128,512]{1,0:T(8,128)(2,1)}) custom-call(s32[1]{0:T(128)} %bitcast.5.here_ref, s32[128,128]{1,0:T(8,128)} %bitcast.10, bf16[3,64,1664]{2,1,0:T(8,128)(2,1)} %bitcast.13, bf16[3,64,1664]{2,1,0:T(8,128)(2,1)} %copy-done.1, bf16[1024,512]{1,0:T(8,128)(2,1)} %constant.32.clone.refs_2_.table_hbm, ...), custom_call_target="tpu_custom_call" | custom-call | flops 999999995904 | bytes 1 | tf_op jit(solution)/shard_map/traces/pallas_call | solution.py:463
  49.1 7.7 %all-to-all-done.1 = bf16[16,32,1920]{2,1,0:T(8,128)(2,1)} async-done(((bf16[16,32,1920]{2,1,0:T(8,128)(2,1)}), bf16[16,32,1920]{2,1,0:T(8,128)(2,1)}, u32[]{:S(2)}, u32[]{:S(2)}) %all-to-all-start.1) | async-done | bytes 1966112 | tf_op jit(solution)/shard_map/all_to_all | solution.py:424
  56.8 8.8 %match.1 = f32[128,256]{1,0:T(8,128)} custom-call(bf16[512,1920]{1,0:T(8,128)(2,1)} %bitcast.4.shapes_hbm, f32[1024,2304]{1,0:T(8,128)} %get-tuple-element.8.kept_hbm, bf16[128,512]{1,0:T(8,128)(2,1)} %get-tuple-element.9.sums_hbm, bf16[1024,512]{1,0:T(8,128)(2,1)} %constant.32.clone.refs_2_.table_hbm), custom_call_target="tpu_custom_call" | custom-call | tf_op jit(solution)/shard_map/match/pallas_call | solution.py:479
  65.6 9.5 %all_to_all.20.parts_ref = f32[16,8,256]{2,1,0:T(8,128)S(1)} all-to-all(f32[16,8,256]{2,1,0:T(8,128)} %bitcast.9), channel_id=1, replica_groups=mesh['half'=2,'deep'=2,'wide'=2,'sta'=2,'core'=2] {'core','sta','wide','..., dimensions={0} | all-to-all | bytes 262144 | tf_op jit(solution)/shard_map/all_to_all | solution.py:424
  75.1 0.6 stack.1
  75.7 10.7 %all_to_all.21 = f32[32,1,256]{2,1,0:T(1,128)S(1)} all-to-all(f32[32,1,256]{2,1,0:T(1,128)S(1)} %get-tuple-element.11), channel_id=1, replica_groups=mesh['half'=2,'deep'=2,'wide'=2,'sta'=2,'core'=2] {'half','deep','wide',..., dimensions={0} | all-to-all | bytes 65536 | tf_op jit(solution)/shard_map/all_to_all | solution.py:424
  86.4 0.6 reduce_max.9
Async XLA Ops:
  0.6 32.5 %collective-permute-start = (bf16[3,64,1664]{2,1,0:T(8,128)(2,1)}, bf16[3,64,1664]{2,1,0:T(8,128)(2,1)S(1)}, u32[]{:S(2)}, u32[]{:S(2)}) collective-permute-start(bf16[3,64,1664]{2,1,0:T(8,128)(2,1)} %bitcast.12), channel_id=1, source_target_pairs={{0,16},{16,0},{1,17},{17,1},{2,18},{18,2},{3,19},{19,3},{4,20},{20... | collective-permute-start | bytes 1916936 | tf_op jit(solution)/shard_map/ppermute | solution.py:432
  6.1 13.3 %all-to-all-start = ((s32[16,8,128]{2,1,0:T(8,128)}), s32[16,8,128]{2,1,0:T(8,128)S(1)}, u32[]{:S(2)}, u32[]{:S(2)}) async-start(s32[16,8,128]{2,1,0:T(8,128)} %lists.1), calls=%async_computation | async-start | bytes 131072 | tf_op jit(solution)/shard_map/all_to_all | solution.py:424
  19.3 0.6 copy-start
  20.0 36.8 %all-to-all-start.1 = ((bf16[16,32,1920]{2,1,0:T(8,128)(2,1)}), bf16[16,32,1920]{2,1,0:T(8,128)(2,1)}, u32[]{:S(2)}, u32[]{:S(2)}) async-start(bf16[16,32,1920]{2,1,0:T(8,128)(2,1)} %bitcast.8), calls=%async_computation.1 | async-start | bytes 3932160 | tf_op jit(solution)/shard_map/all_to_all | solution.py:424
  33.1 0.8 copy-start.1

commit v5 on v4

--- a/solution.py
+++ b/solution.py
@@ -327,7 +327,7 @@
         if part is not None:
             source, buffer = source.at[part], buffer.at[part]
         copies.append(pltpu.make_async_copy(source, buffer, sems.at[len(copies)]))
-        copies[-1].start()
+        copies[-1].start(priority=len(copies) % 2)
         return copies[-1]
 
     lines = [pl.ds(t * packed, packed) for t in range(tiles)]
@@ -499,7 +499,7 @@
         compiler_params=pltpu.CompilerParams(vmem_limit_bytes=16 * MIB),
         name="stack",
     )(parts)
-    return stacks, jnp.max(exchange(top, AXES), axis=(0, 1))
+    return stacks, jnp.max(exchange(top, AXES[::-1]), axis=(0, 1))
 
 
 def solution(mesh):

time: 87.5 us -> 88.8 us (1.015)
  Pallas kernels: 32.3 us -> 33.7 us
    pallas_call x1, Pallas kernels: 8.8 us -> 10.2 us  [body(): pl.pallas_call(functools.partial(match_kernel, cfg, tiles), out_shape=jax...]
where the time goes in v5:
time: 88.8 us; the launch traced here: 88.3 us
  Pallas kernels  33.7 us (38%)
  blocking collectives  20.1 us (23%)
  waiting for transfers between devices  17 us (19%)
  starting transfers between devices  14.7 us (17%)
  local copies, waits for them, and re-layouts  1.45 us (2%)
    all_to_all x2, blocking collectives, exchange(): return lax.all_to_all(x, axes, split_axis=0, concat_axis=0, tiled=True)  20.1 us
    pallas_call x1, Pallas kernels, body(): pl.pallas_call(functools.partial(trace_kernel, cfg), grid=(tiles,), out_s...  15.1 us
    all_to_all x2, starting transfers between devices, exchange(): return lax.all_to_all(x, axes, split_axis=0, concat_axis=0, tiled=True)  10.6 us
    pallas_call x1, Pallas kernels, body(): pl.pallas_call(functools.partial(match_kernel, cfg, tiles), out_shape=jax...  10.2 us
    all_to_all x2, waiting for transfers between devices, exchange(): return lax.all_to_all(x, axes, split_axis=0, concat_axis=0, tiled=True)  9.6 us
    ppermute x1, waiting for transfers between devices, body(): lax.ppermute(waves, HALF, [(0, 1), (1, 0)])  7.36 us
    pallas_call x1, Pallas kernels, body(): pl.pallas_call(functools.partial(pack_kernel, cfg), out_shape=jax.ShapeDt...  6.46 us
    ppermute x1, starting transfers between devices, body(): lax.ppermute(waves, HALF, [(0, 1), (1, 0)])  4.1 us
  transfers between devices with their start and end apart: 3, of which 3 were waited for; matrix products, arithmetic and copies ran while one was open for 0% of the time, Pallas kernels for 26%

profile of v5, /device:TPU:0, one launch (start us, length us, event | category | flops | bytes accessed | tf_op | source)
XLA Modules:
  0.0 88.3 jit_solution(7850146116565277279)
XLA Ops:
  0.6 4.1 %collective-permute-start = (bf16[3,64,1664]{2,1,0:T(8,128)(2,1)}, bf16[3,64,1664]{2,1,0:T(8,128)(2,1)S(1)}, u32[]{:S(2)}, u32[]{:S(2)}) collective-permute-start(bf16[3,64,1664]{2,1,0:T(8,128)(2,1)} %bitcast.12), channel_id=1, source_target_pairs={{0,16},{16,0},{1,17},{17,1},{2,18},{18,2},{3,19},{19,3},{4,20},{20... | collective-permute-start | bytes 1916936 | tf_op jit(solution)/shard_map/ppermute | solution.py:432
  4.7 1.3 %lists.1 = s32[16,8,128]{2,1,0:T(8,128)} custom-call(s32[8,20]{1,0:T(8,128)} %stations_ref.3, s32[8,20]{1,0:T(8,128)} %moveouts_ref.1), custom_call_target="tpu_custom_call" | custom-call | flops 1 | bytes 1 | tf_op jit(solution)/shard_map/lists/pallas_call | solution.py:433
  6.1 4.8 %all-to-all-start = ((s32[16,8,128]{2,1,0:T(8,128)}), s32[16,8,128]{2,1,0:T(8,128)S(1)}, u32[]{:S(2)}, u32[]{:S(2)}) async-start(s32[16,8,128]{2,1,0:T(8,128)} %lists.1), calls=%async_computation | async-start | bytes 131072 | tf_op jit(solution)/shard_map/all_to_all | solution.py:424
  10.9 6.5 %pack.1 = bf16[512,1920]{1,0:T(8,128)(2,1)} custom-call(s32[1]{0:T(128)} %bitcast.1.half_ref, s32[8,20]{1,0:T(8,128)} %stations_ref.3, bf16[20,3,8,1024]{3,2,1,0:T(8,128)(2,1)} %bitcast.11), custom_call_target="tpu_custom_call" | custom-call | flops 5000000000 | bytes 1 | tf_op jit(solution)/shard_map/pack/pallas_call | solution.py:444
  17.4 1.9 %all-to-all-done = s32[16,8,128]{2,1,0:T(8,128)S(1)} async-done(((s32[16,8,128]{2,1,0:T(8,128)}), s32[16,8,128]{2,1,0:T(8,128)S(1)}, u32[]{:S(2)}, u32[]{:S(2)}) %all-to-all-start) | async-done | bytes 65568 | tf_op jit(solution)/shard_map/all_to_all | solution.py:424
  19.3 0.0 copy-start
  19.3 0.6 copy-done
  20.0 5.8 %all-to-all-start.1 = ((bf16[16,32,1920]{2,1,0:T(8,128)(2,1)}), bf16[16,32,1920]{2,1,0:T(8,128)(2,1)}, u32[]{:S(2)}, u32[]{:S(2)}) async-start(bf16[16,32,1920]{2,1,0:T(8,128)(2,1)} %bitcast.8), calls=%async_computation.1 | async-start | bytes 3932160 | tf_op jit(solution)/shard_map/all_to_all | solution.py:424
  25.8 7.4 %collective-permute-done.refs_1_ = bf16[3,64,1664]{2,1,0:T(8,128)(2,1)S(1)} collective-permute-done((bf16[3,64,1664]{2,1,0:T(8,128)(2,1)}, bf16[3,64,1664]{2,1,0:T(8,128)(2,1)S(1)}, u32[]{:S(2)}, u32[]{:S(2)}) %collective-permute-start) | collective-permute-done | bytes 639008 | tf_op jit(solution)/shard_map/ppermute | solution.py:432
  33.1 0.0 copy-start.1
  33.1 0.8 copy-done.1
  34.0 15.1 %traces.1 = (f32[1024,2304]{1,0:T(8,128)}, bf16[128,512]{1,0:T(8,128)(2,1)}) custom-call(s32[1]{0:T(128)} %bitcast.5.here_ref, s32[128,128]{1,0:T(8,128)} %bitcast.10, bf16[3,64,1664]{2,1,0:T(8,128)(2,1)} %bitcast.13, bf16[3,64,1664]{2,1,0:T(8,128)(2,1)} %copy-done.1, bf16[1024,512]{1,0:T(8,128)(2,1)} %constant.32.clone.refs_2_.table_hbm, ...), custom_call_target="tpu_custom_call" | custom-call | flops 999999995904 | bytes 1 | tf_op jit(solution)/shard_map/traces/pallas_call | solution.py:463
  49.1 7.7 %all-to-all-done.1 = bf16[16,32,1920]{2,1,0:T(8,128)(2,1)} async-done(((bf16[16,32,1920]{2,1,0:T(8,128)(2,1)}), bf16[16,32,1920]{2,1,0:T(8,128)(2,1)}, u32[]{:S(2)}, u32[]{:S(2)}) %all-to-all-start.1) | async-done | bytes 1966112 | tf_op jit(solution)/shard_map/all_to_all | solution.py:424
  56.8 10.2 %match.1 = f32[128,256]{1,0:T(8,128)} custom-call(bf16[512,1920]{1,0:T(8,128)(2,1)} %bitcast.4.shapes_hbm, f32[1024,2304]{1,0:T(8,128)} %get-tuple-element.8.kept_hbm, bf16[128,512]{1,0:T(8,128)(2,1)} %get-tuple-element.9.sums_hbm, bf16[1024,512]{1,0:T(8,128)(2,1)} %constant.32.clone.refs_2_.table_hbm), custom_call_target="tpu_custom_call" | custom-call | tf_op jit(solution)/shard_map/match/pallas_call | solution.py:479
  67.0 9.5 %all_to_all.20.parts_ref = f32[16,8,256]{2,1,0:T(8,128)S(1)} all-to-all(f32[16,8,256]{2,1,0:T(8,128)} %bitcast.9), channel_id=1, replica_groups=mesh['half'=2,'deep'=2,'wide'=2,'sta'=2,'core'=2] {'core','sta','wide','..., dimensions={0} | all-to-all | bytes 262144 | tf_op jit(solution)/shard_map/all_to_all | solution.py:424
  76.5 0.6 stack.1
  77.1 10.6 %all_to_all.21 = f32[32,1,256]{2,1,0:T(1,128)S(1)} all-to-all(f32[32,1,256]{2,1,0:T(1,128)S(1)} %get-tuple-element.11), channel_id=1, replica_groups=mesh['half'=2,'deep'=2,'wide'=2,'sta'=2,'core'=2] {'core','sta','wide','..., dimensions={0} | all-to-all | bytes 65536 | tf_op jit(solution)/shard_map/all_to_all | solution.py:424
  87.7 0.6 reduce_max.9
Async XLA Ops:
  0.6 32.5 %collective-permute-start = (bf16[3,64,1664]{2,1,0:T(8,128)(2,1)}, bf16[3,64,1664]{2,1,0:T(8,128)(2,1)S(1)}, u32[]{:S(2)}, u32[]{:S(2)}) collective-permute-start(bf16[3,64,1664]{2,1,0:T(8,128)(2,1)} %bitcast.12), channel_id=1, source_target_pairs={{0,16},{16,0},{1,17},{17,1},{2,18},{18,2},{3,19},{19,3},{4,20},{20... | collective-permute-start | bytes 1916936 | tf_op jit(solution)/shard_map/ppermute | solution.py:432
  6.1 13.3 %all-to-all-start = ((s32[16,8,128]{2,1,0:T(8,128)}), s32[16,8,128]{2,1,0:T(8,128)S(1)}, u32[]{:S(2)}, u32[]{:S(2)}) async-start(s32[16,8,128]{2,1,0:T(8,128)} %lists.1), calls=%async_computation | async-start | bytes 131072 | tf_op jit(solution)/shard_map/all_to_all | solution.py:424
  19.3 0.6 copy-start
  20.0 36.8 %all-to-all-start.1 = ((bf16[16,32,1920]{2,1,0:T(8,128)(2,1)}), bf16[16,32,1920]{2,1,0:T(8,128)(2,1)}, u32[]{:S(2)}, u32[]{:S(2)}) async-start(bf16[16,32,1920]{2,1,0:T(8,128)(2,1)} %bitcast.8), calls=%async_computation.1 | async-start | bytes 3932160 | tf_op jit(solution)/shard_map/all_to_all | solution.py:424
  33.1 0.8 copy-start.1

commit v6 on v4

--- a/solution.py
+++ b/solution.py
@@ -332,18 +332,21 @@
 
     lines = [pl.ds(t * packed, packed) for t in range(tiles)]
     halves = [pl.ds(q * 2 * LAGS, 2 * LAGS) for q in range(2)]
+    part = tile // 2
+
+    def fetch_kept(t, k):
+        return fetch(kept_hbm, kept_ref, pl.ds(t * tile + k * part, part))
+
     forward = fetch(table_hbm, table_ref, halves[0])
-    part = tile // 2
-    shapes, kept = [], []
+    shapes = fetch(shapes_hbm, shapes_ref, lines[0])
+    kept = [fetch_kept(0, 0)]
+    forward.wait()
     for t in range(tiles):
-        shapes.append(fetch(shapes_hbm, shapes_ref, lines[t]))
-        kept.append([fetch(kept_hbm, kept_ref, pl.ds(t * tile + k * part, part)) for k in range(2)])
+        shapes.wait()
         if t == 0:
+            kept.append(fetch_kept(0, 1))
             inverse = fetch(table_hbm, table_ref, halves[1])
             sums = fetch(sums_hbm, sums_ref)
-    forward.wait()
-    for t in range(tiles):
-        shapes[t].wait()
         mine = shape_spectra(line_pieces(cfg, shapes_ref[lines[t], :]), table_ref[: 2 * LAGS, :])
         if t == 0:
             for copy in (inverse, sums):
@@ -351,7 +354,11 @@
         ends = pl.ds(t * groups, groups)
         total = 0.0
         for k in range(2):
-            kept[t][k].wait()
+            kept[2 * t + k].wait()
+            if t + 1 < tiles:
+                if k == 0:
+                    shapes = fetch(shapes_hbm, shapes_ref, lines[t + 1])
+                kept.append(fetch_kept(t + 1, k))
             theirs = kept_ref[pl.ds(t * tile + k * part, part), :]
             spectra = [
                 (theirs[:, 2 * h * LAGS : (2 * h + 1) * LAGS], theirs[:, (2 * h + 1) * LAGS : (2 * h + 2) * LAGS])

time: 87.5 us -> 87.9 us (level)
  no operation moved by 1% of the time
where the time goes in v6:
time: 87.9 us; the launch traced here: 87.4 us
  Pallas kernels  32.8 us (37%)
  blocking collectives  20.2 us (23%)
  waiting for transfers between devices  17 us (19%)
  starting transfers between devices  14.7 us (17%)
  local copies, waits for them, and re-layouts  1.45 us (2%)
    all_to_all x2, blocking collectives, exchange(): return lax.all_to_all(x, axes, split_axis=0, concat_axis=0, tiled=True)  20.2 us
    pallas_call x1, Pallas kernels, body(): pl.pallas_call(functools.partial(trace_kernel, cfg), grid=(tiles,), out_s...  15.1 us
    all_to_all x2, starting transfers between devices, exchange(): return lax.all_to_all(x, axes, split_axis=0, concat_axis=0, tiled=True)  10.6 us
    all_to_all x2, waiting for transfers between devices, exchange(): return lax.all_to_all(x, axes, split_axis=0, concat_axis=0, tiled=True)  9.6 us
    pallas_call x1, Pallas kernels, body(): pl.pallas_call(functools.partial(match_kernel, cfg, tiles), out_shape=jax...  9.23 us
    ppermute x1, waiting for transfers between devices, body(): lax.ppermute(waves, HALF, [(0, 1), (1, 0)])  7.36 us
    pallas_call x1, Pallas kernels, body(): pl.pallas_call(functools.partial(pack_kernel, cfg), out_shape=jax.ShapeDt...  6.46 us
    ppermute x1, starting transfers between devices, body(): lax.ppermute(waves, HALF, [(0, 1), (1, 0)])  4.1 us
  transfers between devices with their start and end apart: 3, of which 3 were waited for; matrix products, arithmetic and copies ran while one was open for 0% of the time, Pallas kernels for 26%

profile of v6, /device:TPU:0, one launch (start us, length us, event | category | flops | bytes accessed | tf_op | source)
XLA Modules:
  0.0 87.4 jit_solution(17400997234245481572)
XLA Ops:
  0.6 4.1 %collective-permute-start = (bf16[3,64,1664]{2,1,0:T(8,128)(2,1)}, bf16[3,64,1664]{2,1,0:T(8,128)(2,1)S(1)}, u32[]{:S(2)}, u32[]{:S(2)}) collective-permute-start(bf16[3,64,1664]{2,1,0:T(8,128)(2,1)} %bitcast.12), channel_id=1, source_target_pairs={{0,16},{16,0},{1,17},{17,1},{2,18},{18,2},{3,19},{19,3},{4,20},{20... | collective-permute-start | bytes 1916936 | tf_op jit(solution)/shard_map/ppermute | solution.py:439
  4.7 1.3 %lists.1 = s32[16,8,128]{2,1,0:T(8,128)} custom-call(s32[8,20]{1,0:T(8,128)} %stations_ref.3, s32[8,20]{1,0:T(8,128)} %moveouts_ref.1), custom_call_target="tpu_custom_call" | custom-call | flops 1 | bytes 1 | tf_op jit(solution)/shard_map/lists/pallas_call | solution.py:440
  6.1 4.8 %all-to-all-start = ((s32[16,8,128]{2,1,0:T(8,128)}), s32[16,8,128]{2,1,0:T(8,128)S(1)}, u32[]{:S(2)}, u32[]{:S(2)}) async-start(s32[16,8,128]{2,1,0:T(8,128)} %lists.1), calls=%async_computation | async-start | bytes 131072 | tf_op jit(solution)/shard_map/all_to_all | solution.py:431
  10.9 6.5 %pack.1 = bf16[512,1920]{1,0:T(8,128)(2,1)} custom-call(s32[1]{0:T(128)} %bitcast.1.half_ref, s32[8,20]{1,0:T(8,128)} %stations_ref.3, bf16[20,3,8,1024]{3,2,1,0:T(8,128)(2,1)} %bitcast.11), custom_call_target="tpu_custom_call" | custom-call | flops 5000000000 | bytes 1 | tf_op jit(solution)/shard_map/pack/pallas_call | solution.py:451
  17.4 1.9 %all-to-all-done = s32[16,8,128]{2,1,0:T(8,128)S(1)} async-done(((s32[16,8,128]{2,1,0:T(8,128)}), s32[16,8,128]{2,1,0:T(8,128)S(1)}, u32[]{:S(2)}, u32[]{:S(2)}) %all-to-all-start) | async-done | bytes 65568 | tf_op jit(solution)/shard_map/all_to_all | solution.py:431
  19.3 0.0 copy-start
  19.3 0.6 copy-done
  20.0 5.8 %all-to-all-start.1 = ((bf16[16,32,1920]{2,1,0:T(8,128)(2,1)}), bf16[16,32,1920]{2,1,0:T(8,128)(2,1)}, u32[]{:S(2)}, u32[]{:S(2)}) async-start(bf16[16,32,1920]{2,1,0:T(8,128)(2,1)} %bitcast.8), calls=%async_computation.1 | async-start | bytes 3932160 | tf_op jit(solution)/shard_map/all_to_all | solution.py:431
  25.8 7.4 %collective-permute-done.refs_1_ = bf16[3,64,1664]{2,1,0:T(8,128)(2,1)S(1)} collective-permute-done((bf16[3,64,1664]{2,1,0:T(8,128)(2,1)}, bf16[3,64,1664]{2,1,0:T(8,128)(2,1)S(1)}, u32[]{:S(2)}, u32[]{:S(2)}) %collective-permute-start) | collective-permute-done | bytes 639008 | tf_op jit(solution)/shard_map/ppermute | solution.py:439
  33.1 0.0 copy-start.1
  33.1 0.8 copy-done.1
  34.0 15.1 %traces.1 = (f32[1024,2304]{1,0:T(8,128)}, bf16[128,512]{1,0:T(8,128)(2,1)}) custom-call(s32[1]{0:T(128)} %bitcast.5.here_ref, s32[128,128]{1,0:T(8,128)} %bitcast.10, bf16[3,64,1664]{2,1,0:T(8,128)(2,1)} %bitcast.13, bf16[3,64,1664]{2,1,0:T(8,128)(2,1)} %copy-done.1, bf16[1024,512]{1,0:T(8,128)(2,1)} %constant.32.clone.refs_2_.table_hbm, ...), custom_call_target="tpu_custom_call" | custom-call | flops 999999995904 | bytes 1 | tf_op jit(solution)/shard_map/traces/pallas_call | solution.py:470
  49.1 7.7 %all-to-all-done.1 = bf16[16,32,1920]{2,1,0:T(8,128)(2,1)} async-done(((bf16[16,32,1920]{2,1,0:T(8,128)(2,1)}), bf16[16,32,1920]{2,1,0:T(8,128)(2,1)}, u32[]{:S(2)}, u32[]{:S(2)}) %all-to-all-start.1) | async-done | bytes 1966112 | tf_op jit(solution)/shard_map/all_to_all | solution.py:431
  56.8 9.2 %match.1 = f32[128,256]{1,0:T(8,128)} custom-call(bf16[512,1920]{1,0:T(8,128)(2,1)} %bitcast.4.shapes_hbm, f32[1024,2304]{1,0:T(8,128)} %get-tuple-element.8.kept_hbm, bf16[128,512]{1,0:T(8,128)(2,1)} %get-tuple-element.9.sums_hbm, bf16[1024,512]{1,0:T(8,128)(2,1)} %constant.32.clone.refs_2_.table_hbm), custom_call_target="tpu_custom_call" | custom-call | tf_op jit(solution)/shard_map/match/pallas_call | solution.py:486
  66.0 9.5 %all_to_all.20.parts_ref = f32[16,8,256]{2,1,0:T(8,128)S(1)} all-to-all(f32[16,8,256]{2,1,0:T(8,128)} %bitcast.9), channel_id=1, replica_groups=mesh['half'=2,'deep'=2,'wide'=2,'sta'=2,'core'=2] {'core','sta','wide','..., dimensions={0} | all-to-all | bytes 262144 | tf_op jit(solution)/shard_map/all_to_all | solution.py:431
  75.5 0.6 stack.1
  76.1 10.7 %all_to_all.21 = f32[32,1,256]{2,1,0:T(1,128)S(1)} all-to-all(f32[32,1,256]{2,1,0:T(1,128)S(1)} %get-tuple-element.11), channel_id=1, replica_groups=mesh['half'=2,'deep'=2,'wide'=2,'sta'=2,'core'=2] {'half','deep','wide',..., dimensions={0} | all-to-all | bytes 65536 | tf_op jit(solution)/shard_map/all_to_all | solution.py:431
  86.8 0.6 reduce_max.9
Async XLA Ops:
  0.6 32.5 %collective-permute-start = (bf16[3,64,1664]{2,1,0:T(8,128)(2,1)}, bf16[3,64,1664]{2,1,0:T(8,128)(2,1)S(1)}, u32[]{:S(2)}, u32[]{:S(2)}) collective-permute-start(bf16[3,64,1664]{2,1,0:T(8,128)(2,1)} %bitcast.12), channel_id=1, source_target_pairs={{0,16},{16,0},{1,17},{17,1},{2,18},{18,2},{3,19},{19,3},{4,20},{20... | collective-permute-start | bytes 1916936 | tf_op jit(solution)/shard_map/ppermute | solution.py:439
  6.1 13.3 %all-to-all-start = ((s32[16,8,128]{2,1,0:T(8,128)}), s32[16,8,128]{2,1,0:T(8,128)S(1)}, u32[]{:S(2)}, u32[]{:S(2)}) async-start(s32[16,8,128]{2,1,0:T(8,128)} %lists.1), calls=%async_computation | async-start | bytes 131072 | tf_op jit(solution)/shard_map/all_to_all | solution.py:431
  19.3 0.6 copy-start
  20.0 36.8 %all-to-all-start.1 = ((bf16[16,32,1920]{2,1,0:T(8,128)(2,1)}), bf16[16,32,1920]{2,1,0:T(8,128)(2,1)}, u32[]{:S(2)}, u32[]{:S(2)}) async-start(bf16[16,32,1920]{2,1,0:T(8,128)(2,1)} %bitcast.8), calls=%async_computation.1 | async-start | bytes 3932160 | tf_op jit(solution)/shard_map/all_to_all | solution.py:431
  33.1 0.8 copy-start.1

commit v7 on v4

--- a/solution.py
+++ b/solution.py
@@ -483,7 +483,7 @@
         out_specs=whole,
         scratch_shapes=[pltpu.VMEM(x.shape, x.dtype) for x in operands]
         + [pltpu.SemaphoreType.DMA((3 + 3 * tiles,))],
-        compiler_params=pltpu.CompilerParams(vmem_limit_bytes=57 * MIB),
+        compiler_params=pltpu.CompilerParams(vmem_limit_bytes=40 * MIB),
         name="match",
     )(*operands)
 

time: 87.5 us -> 91 us (1.040)
  local copies, waits for them, and re-layouts: 1.45 us -> 6.02 us
    unnamed x4 -> x10, local copies, waits for them, and re-layouts: 1.45 us -> 6.02 us
  transfers between devices with their start and end apart: 3 -> 3, of which waited for: 3 -> 3; matrix products, arithmetic and copies ran while one was open for 0% -> 0% of each run, Pallas kernels for 26% -> 25%
where the time goes in v7:
time: 91 us; the launch traced here: 90.6 us
  Pallas kernels  31.7 us (35%)
  blocking collectives  20 us (22%)
  waiting for transfers between devices  16.8 us (18%)
  starting transfers between devices  14.7 us (16%)
  local copies, waits for them, and re-layouts  6.02 us (7%)
    all_to_all x2, blocking collectives, exchange(): return lax.all_to_all(x, axes, split_axis=0, concat_axis=0, tiled=True)  20 us
    pallas_call x1, Pallas kernels, body(): pl.pallas_call(functools.partial(trace_kernel, cfg), grid=(tiles,), out_s...  15.2 us
    all_to_all x2, starting transfers between devices, exchange(): return lax.all_to_all(x, axes, split_axis=0, concat_axis=0, tiled=True)  10.6 us
    all_to_all x2, waiting for transfers between devices, exchange(): return lax.all_to_all(x, axes, split_axis=0, concat_axis=0, tiled=True)  9.47 us
    pallas_call x1, Pallas kernels, body(): pl.pallas_call(functools.partial(match_kernel, cfg, tiles), out_shape=jax...  8 us
    ppermute x1, waiting for transfers between devices, body(): lax.ppermute(waves, HALF, [(0, 1), (1, 0)])  7.36 us
    pallas_call x1, Pallas kernels, body(): pl.pallas_call(functools.partial(pack_kernel, cfg), out_shape=jax.ShapeDt...  6.52 us
    unnamed x10, local copies, waits for them, and re-layouts  6.02 us
  transfers between devices with their start and end apart: 3, of which 3 were waited for; matrix products, arithmetic and copies ran while one was open for 0% of the time, Pallas kernels for 25%

profile of v7, /device:TPU:0, one launch (start us, length us, event | category | flops | bytes accessed | tf_op | source)
XLA Modules:
  0.0 90.6 jit_solution(601181369323927332)
XLA Ops:
  0.6 4.1 %collective-permute-start = (bf16[3,64,1664]{2,1,0:T(8,128)(2,1)}, bf16[3,64,1664]{2,1,0:T(8,128)(2,1)S(1)}, u32[]{:S(2)}, u32[]{:S(2)}) collective-permute-start(bf16[3,64,1664]{2,1,0:T(8,128)(2,1)} %bitcast.12), channel_id=1, source_target_pairs={{0,16},{16,0},{1,17},{17,1},{2,18},{18,2},{3,19},{19,3},{4,20},{20... | collective-permute-start | bytes 1916936 | tf_op jit(solution)/shard_map/ppermute | solution.py:432
  4.7 1.3 %lists.1 = s32[16,8,128]{2,1,0:T(8,128)} custom-call(s32[8,20]{1,0:T(8,128)} %stations_ref.3, s32[8,20]{1,0:T(8,128)} %moveouts_ref.1), custom_call_target="tpu_custom_call" | custom-call | flops 1 | bytes 1 | tf_op jit(solution)/shard_map/lists/pallas_call | solution.py:433
  6.1 4.8 %all-to-all-start = ((s32[16,8,128]{2,1,0:T(8,128)}), s32[16,8,128]{2,1,0:T(8,128)S(1)}, u32[]{:S(2)}, u32[]{:S(2)}) async-start(s32[16,8,128]{2,1,0:T(8,128)} %lists.1), calls=%async_computation | async-start | bytes 131072 | tf_op jit(solution)/shard_map/all_to_all | solution.py:424
  10.9 6.5 %pack.1 = bf16[512,1920]{1,0:T(8,128)(2,1)} custom-call(s32[1]{0:T(128)} %bitcast.1.half_ref, s32[8,20]{1,0:T(8,128)} %stations_ref.3, bf16[20,3,8,1024]{3,2,1,0:T(8,128)(2,1)} %bitcast.11), custom_call_target="tpu_custom_call" | custom-call | flops 5000000000 | bytes 1 | tf_op jit(solution)/shard_map/pack/pallas_call | solution.py:444
  17.5 1.9 %all-to-all-done = s32[16,8,128]{2,1,0:T(8,128)S(1)} async-done(((s32[16,8,128]{2,1,0:T(8,128)}), s32[16,8,128]{2,1,0:T(8,128)S(1)}, u32[]{:S(2)}, u32[]{:S(2)}) %all-to-all-start) | async-done | bytes 65568 | tf_op jit(solution)/shard_map/all_to_all | solution.py:424
  19.3 0.0 copy-start.3
  19.3 0.6 copy-done.3
  20.0 5.8 %all-to-all-start.1 = ((bf16[16,32,1920]{2,1,0:T(8,128)(2,1)}), bf16[16,32,1920]{2,1,0:T(8,128)(2,1)}, u32[]{:S(2)}, u32[]{:S(2)}) async-start(bf16[16,32,1920]{2,1,0:T(8,128)(2,1)} %bitcast.9), calls=%async_computation.1 | async-start | bytes 3932160 | tf_op jit(solution)/shard_map/all_to_all | solution.py:424
  25.8 7.4 %collective-permute-done.refs_1_ = bf16[3,64,1664]{2,1,0:T(8,128)(2,1)S(1)} collective-permute-done((bf16[3,64,1664]{2,1,0:T(8,128)(2,1)}, bf16[3,64,1664]{2,1,0:T(8,128)(2,1)S(1)}, u32[]{:S(2)}, u32[]{:S(2)}) %collective-permute-start) | collective-permute-done | bytes 639008 | tf_op jit(solution)/shard_map/ppermute | solution.py:432
  33.1 0.0 copy-start.4
  33.1 0.8 copy-done.4
  33.9 0.0 copy-start.1
  33.9 15.2 %traces.1 = (f32[1024,2304]{1,0:T(8,128)}, bf16[128,512]{1,0:T(8,128)(2,1)}) custom-call(s32[1]{0:T(128)} %bitcast.5.here_ref, s32[128,128]{1,0:T(8,128)} %bitcast.10, bf16[3,64,1664]{2,1,0:T(8,128)(2,1)} %bitcast.13, bf16[3,64,1664]{2,1,0:T(8,128)(2,1)} %copy-done.4, bf16[1024,512]{1,0:T(8,128)(2,1)} %constant.32.clone.refs_2_.table_hbm, ...), custom_call_target="tpu_custom_call" | custom-call | flops 999999995904 | bytes 1 | tf_op jit(solution)/shard_map/traces/pallas_call | solution.py:463
  49.1 7.6 %all-to-all-done.1 = bf16[16,32,1920]{2,1,0:T(8,128)(2,1)} async-done(((bf16[16,32,1920]{2,1,0:T(8,128)(2,1)}), bf16[16,32,1920]{2,1,0:T(8,128)(2,1)}, u32[]{:S(2)}, u32[]{:S(2)}) %all-to-all-start.1) | async-done | bytes 1966112 | tf_op jit(solution)/shard_map/all_to_all | solution.py:424
  56.8 0.0 copy-done.1
  56.8 0.0 copy-start
  56.8 3.7 %copy-done = f32[1024,2304]{1,0:T(8,128)S(1)} copy-done((f32[1024,2304]{1,0:T(8,128)S(1)}, f32[1024,2304]{1,0:T(8,128)}, u32[]{:S(2)}) %copy-start) | copy-done | bytes 9437208
  60.4 0.0 copy-start.2
  60.4 0.9 copy-done.2
  61.3 8.0 %match.1 = f32[128,256]{1,0:T(8,128)S(1)} custom-call(bf16[512,1920]{1,0:T(8,128)(2,1)} %bitcast.4.shapes_hbm, f32[1024,2304]{1,0:T(8,128)S(1)} %copy-done, bf16[128,512]{1,0:T(8,128)(2,1)S(1)} %copy-done.2, bf16[1024,512]{1,0:T(8,128)(2,1)S(1)} %copy-done.1), custom_call_target="tpu_custom_call" | custom-call | tf_op jit(solution)/shard_map/match/pallas_call | solution.py:479
  69.4 8.7 %all_to_all.20.parts_ref = f32[16,8,256]{2,1,0:T(8,128)S(1)} all-to-all(f32[16,8,256]{2,1,0:T(8,128)S(1)} %bitcast.8), channel_id=1, replica_groups=mesh['half'=2,'deep'=2,'wide'=2,'sta'=2,'core'=2] {'core','sta','wide','..., dimensions={0} | all-to-all | bytes 262144 | tf_op jit(solution)/shard_map/all_to_all | solution.py:424
  78.0 0.6 stack.1
  78.6 11.3 %all_to_all.21 = f32[32,1,256]{2,1,0:T(1,128)S(1)} all-to-all(f32[32,1,256]{2,1,0:T(1,128)S(1)} %get-tuple-element.11), channel_id=1, replica_groups=mesh['half'=2,'deep'=2,'wide'=2,'sta'=2,'core'=2] {'half','deep','wide',..., dimensions={0} | all-to-all | bytes 65536 | tf_op jit(solution)/shard_map/all_to_all | solution.py:424
  89.9 0.6 reduce_max.9
Async XLA Ops:
  0.6 32.5 %collective-permute-start = (bf16[3,64,1664]{2,1,0:T(8,128)(2,1)}, bf16[3,64,1664]{2,1,0:T(8,128)(2,1)S(1)}, u32[]{:S(2)}, u32[]{:S(2)}) collective-permute-start(bf16[3,64,1664]{2,1,0:T(8,128)(2,1)} %bitcast.12), channel_id=1, source_target_pairs={{0,16},{16,0},{1,17},{17,1},{2,18},{18,2},{3,19},{19,3},{4,20},{20... | collective-permute-start | bytes 1916936 | tf_op jit(solution)/shard_map/ppermute | solution.py:432
  6.1 13.3 %all-to-all-start = ((s32[16,8,128]{2,1,0:T(8,128)}), s32[16,8,128]{2,1,0:T(8,128)S(1)}, u32[]{:S(2)}, u32[]{:S(2)}) async-start(s32[16,8,128]{2,1,0:T(8,128)} %lists.1), calls=%async_computation | async-start | bytes 131072 | tf_op jit(solution)/shard_map/all_to_all | solution.py:424
  19.3 0.6 copy-start.3
  20.0 36.8 %all-to-all-start.1 = ((bf16[16,32,1920]{2,1,0:T(8,128)(2,1)}), bf16[16,32,1920]{2,1,0:T(8,128)(2,1)}, u32[]{:S(2)}, u32[]{:S(2)}) async-start(bf16[16,32,1920]{2,1,0:T(8,128)(2,1)} %bitcast.9), calls=%async_computation.1 | async-start | bytes 3932160 | tf_op jit(solution)/shard_map/all_to_all | solution.py:424
  33.1 0.8 copy-start.4
  33.9 22.8 %copy-start.1 = (bf16[1024,512]{1,0:T(8,128)(2,1)S(1)}, bf16[1024,512]{1,0:T(8,128)(2,1)}, u32[]{:S(2)}) copy-start(bf16[1024,512]{1,0:T(8,128)(2,1)} %constant.32.clone.refs_2_.table_hbm) | copy-start | bytes 3145732
  56.8 3.7 %copy-start = (f32[1024,2304]{1,0:T(8,128)S(1)}, f32[1024,2304]{1,0:T(8,128)}, u32[]{:S(2)}) copy-start(f32[1024,2304]{1,0:T(8,128)} %get-tuple-element.8.kept_hbm) | copy-start | bytes 28311556
  60.4 0.9 copy-start.2
